TPU v7x, 32 devices: a whole 2x2x4 slice. The times are simulated.
32 devices in a mesh: dp: 16 (over z, x, core), feat: 2 (over y).
Axes of the slice: x: 2, y: 2, z: 4, core: 2. Of those that a mesh axis runs over, the one named last changes fastest.
Arguments:
- proj_grads: bfloat16 [4096, 16384], P('dp', 'feat'), may hold values from -1.25 to 1.25
- val_grads: bfloat16 [16384, 128], P('feat'), may hold values from -1.25 to 1.25
Outputs:
- interactions: bfloat16 [4096, 4096], P('dp', 'feat')
- data_scores: float32 [4096, 128], P('dp')
All inputs are finite; a program needn't handle non-finite values.
Results may differ from a plain program's by a relative error of at most 0.0006.
Values may be sent and summed in bfloat16 or wider, within the bound.
A program may use at most 192 MiB of HBM per device.

v0:
```python
import jax
import jax.numpy as jnp
from jax import lax
from jax.sharding import PartitionSpec as P


def pair_tile(left_rows, right_rows):
    return lax.dot_general(
        left_rows, right_rows, (((1,), (1,)), ((), ())), preferred_element_type=jnp.float32
    )


def body(proj_grads, val_grads):
    row_count = proj_grads.shape[0]
    pair_weight = 1.0 / row_count**0.5
    dp_index = lax.axis_index("dp")
    feat_index = lax.axis_index("feat")
    first_local = lax.psum(
        jnp.dot(proj_grads, val_grads, preferred_element_type=jnp.float32), "feat"
    )
    block_row = pair_tile(proj_grads, lax.all_gather(proj_grads, "dp", axis=0, tiled=True))
    gram_cols = lax.psum_scatter(block_row, "feat", scatter_dimension=1, tiled=True)
    col_count = gram_cols.shape[1]
    row_ids = dp_index * row_count + jnp.arange(row_count, dtype=jnp.int32)
    col_ids = feat_index * col_count + jnp.arange(col_count, dtype=jnp.int32)
    pair_values = jnp.where(row_ids[:, None] == col_ids[None, :], 0.0, gram_cols)
    first_all = lax.all_gather(first_local, "dp", axis=0, tiled=True)
    first_cols = lax.dynamic_slice_in_dim(first_all, feat_index * col_count, col_count, 0)
    partial_sum = jnp.dot(pair_values, first_cols, precision=lax.Precision.HIGHEST)
    pair_sum = lax.psum(partial_sum, "feat")
    data_scores = first_local - pair_weight * pair_sum
    return (pair_values.astype(jnp.bfloat16), data_scores)


def solution(mesh):
    return jax.shard_map(
        body,
        mesh=mesh,
        in_specs=(P("dp", "feat"), P("feat", None)),
        out_specs=(P("dp", "feat"), P("dp", None)),
        check_vma=False,
    )
```

profile of v0, /device:TPU:18, one launch (start us, length us, event | category | flops | bytes accessed | tf_op | source)
XLA Modules:
  0.0 461.4 jit_solution(7305637518699466460)
XLA Ops:
  8.0 0.0 copy-start
  8.0 0.0 all-reduce.3.cloned.1.call-start
  8.1 1.5 copy-done
  9.6 4.1 fusion.9
  13.7 0.0 all-reduce.3.cloned.1.call-update
  13.7 0.0 all-gather.3.cloned.1.call-start
  13.8 0.5 all-gather.3.cloned.1.call-update
  14.3 0.0 all-gather.5.cloned.1.call-start
  14.3 22.0 %all-reduce.3.cloned.1.call-done = f32[256,128]{1,0:T(8,128)} async-done(((f32[256,128]{1,0:T(8,128)}), f32[256,128]{1,0:T(8,128)}) %all-reduce.3.cloned.1.call-update) | async-done | bytes 131088 | tf_op jit(solution)/shard_map/psum | solution.py:18
  36.3 0.0 all-gather.5.cloned.1.call-update
  36.4 0.0 reduce-scatter.2.cloned.1.call-start
  36.4 305.8 %all-gather.3.cloned.1.call-done = bf16[4096,8192]{1,0:T(8,128)(2,1)} async-done(((bf16[256,8192]{1,0:T(8,128)(2,1)}), bf16[4096,8192]{1,0:T(8,128)(2,1)}) %all-gather.3.cloned.1.call-update) | async-done | bytes 67108880 | tf_op jit(solution)/shard_map/all_gather | solution.py:21
  342.2 29.3 %fusion.8 = f32[256,4096]{1,0:T(8,128)} fusion(bf16[256,8192]{1,0:T(8,128)(2,1)} %param.2, bf16[4096,8192]{1,0:T(8,128)(2,1)} %all-gather.3.cloned.1.call-done), kind=kOutput, calls=%fused_computation.12 | convolution fusion | flops 17179869184 | bytes 75497472 | tf_op jit(solution)/shard_map/dot_general | solution.py:8
  371.5 0.0 reduce-scatter.2.cloned.1.call-update
  371.6 0.0 all-reduce.5.cloned.1.call-start
  371.6 12.4 %all-gather.5.cloned.1.call-done = f32[4096,128]{1,0:T(8,128)} async-done(((f32[256,128]{1,0:T(8,128)}), f32[4096,128]{1,0:T(8,128)}) %all-gather.5.cloned.1.call-update) | async-done | bytes 2097168 | tf_op jit(solution)/shard_map/all_gather | solution.py:27
  384.0 42.7 %reduce-scatter.2.cloned.1.call-done = f32[256,2048]{1,0:T(8,128)} async-done(((f32[256,4096]{1,0:T(8,128)}), f32[256,2048]{1,0:T(8,128)}) %reduce-scatter.2.cloned.1.call-update) | async-done | bytes 2097168 | tf_op jit(solution)/shard_map/reduce_scatter | solution.py:22
  426.7 4.4 fusion
  431.1 0.0 copy-start.1
  431.1 0.0 all-reduce.5.cloned.1.call-update
  431.1 2.8 fusion.1
  434.0 18.8 %all-reduce.5.cloned.1.call-done = f32[256,128]{1,0:T(8,128)} async-done(((f32[256,128]{1,0:T(8,128)}), f32[256,128]{1,0:T(8,128)}) %all-reduce.5.cloned.1.call-update) | async-done | bytes 131088 | tf_op jit(solution)/shard_map/psum | solution.py:30
  452.7 0.0 copy-done.1
  452.7 1.6 multiply_subtract_fusion
  (2 shorter events, 0.0 us)
Async XLA Ops:
  8.0 1.6 copy-start
  8.0 28.3 %all-reduce.3.cloned.1.call-start = ((), (), s32[]{:S(2)}) async-start(), calls=%async_computation.3 | async-start | bytes 262144 | tf_op jit(solution)/shard_map/psum | solution.py:18
  13.7 328.5 %all-gather.3.cloned.1.call-start = ((), (), s32[]{:S(2)}) async-start(), calls=%async_computation.1 | async-start | bytes 71303168 | tf_op jit(solution)/shard_map/all_gather | solution.py:21
  14.3 369.8 %all-gather.5.cloned.1.call-start = ((), (), s32[]{:S(2)}) async-start(), calls=%async_computation.4 | async-start | bytes 2228224 | tf_op jit(solution)/shard_map/all_gather | solution.py:27
  36.4 390.3 %reduce-scatter.2.cloned.1.call-start = ((), (), s32[]{:S(2)}) async-start(), calls=%async_computation.2 | async-start | bytes 6291456 | tf_op jit(solution)/shard_map/reduce_scatter | solution.py:22
  371.6 81.2 %all-reduce.5.cloned.1.call-start = ((), (), s32[]{:S(2)}) async-start(), calls=%async_computation.5 | async-start | bytes 262144 | tf_op jit(solution)/shard_map/psum | solution.py:30
  431.1 21.6 %copy-start.1 = (f32[256,128]{1,0:T(8,128)S(1)}, f32[256,128]{1,0:T(8,128)}, u32[]{:S(2)}) copy-start(f32[256,128]{1,0:T(8,128)} %all-reduce.3.cloned.1.call-done) | copy-start | bytes 393220
Sparse Core Ops, SparseCore 0:
  13.8 22.4 all-reduce.2
  371.7 54.9 reduce-scatter.1
  431.3 21.4 all-reduce.4
Sparse Core Ops, SparseCore 1:
  15.8 326.4 all-gather.2
  344.5 39.5 all-gather.4
where the time goes:
time: 463 us; the launch traced here: 461 us
  waiting for transfers between devices  402 us (87%)
  matrix products  37.8 us (8%)
  between operations  15.2 us (3%)
    all_gather x1, waiting for transfers between devices, body(): lax.all_gather(proj_grads, 'dp', axis=0, tiled=True)  306 us
    reduce_scatter x1, waiting for transfers between devices, body(): lax.psum_scatter(block_row, 'feat', scatter_dimension=1, tiled=True)  42.7 us
    dot_general x1, matrix products, pair_tile(): lax.dot_general(left_rows, right_rows, (((1,), (1,)), ((), ())), preferre...  29.3 us
    psum x1, waiting for transfers between devices, body(): lax.psum(jnp.dot(proj_grads, val_grads, preferred_element_type=jnp.float3...  22 us
    psum x1, waiting for transfers between devices, body(): pair_sum = lax.psum(partial_sum, 'feat')  18.8 us
    all_gather x1, waiting for transfers between devices, body(): first_all = lax.all_gather(first_local, 'dp', axis=0, tiled=True)  12.4 us
  transfers between devices with their start and end apart: 5, of which 5 were waited for; matrix products, arithmetic and copies ran while one was open for 7% of the time, Pallas kernels for 0%

commit v1 on v0

--- a/solution.py
+++ b/solution.py
@@ -1,3 +1,5 @@
+import functools
+
 import jax
 import jax.numpy as jnp
 from jax import lax
@@ -10,7 +12,7 @@
     )
 
 
-def body(proj_grads, val_grads):
+def general_body(proj_grads, val_grads):
     row_count = proj_grads.shape[0]
     pair_weight = 1.0 / row_count**0.5
     dp_index = lax.axis_index("dp")
@@ -32,7 +34,80 @@
     return (pair_values.astype(jnp.bfloat16), data_scores)
 
 
+KEPT = ((0, 1), (2, 3), (1, 0), (2, 3))
+
+
+def split_body(n_dp, proj_grads, val_grads):
+    per_part = n_dp // 4
+    half = n_dp // 2
+    row_count = proj_grads.shape[0]
+    pair_weight = 1.0 / row_count**0.5
+    dp_index = lax.axis_index("dp")
+    feat_index = lax.axis_index("feat")
+    part = dp_index // per_part
+    inner = dp_index % per_part
+    both = ("dp", "feat")
+
+    def flat(part, inner, feat):
+        return (part * per_part + inner) * 2 + feat
+
+    def fetch(which):
+        return [
+            (flat(KEPT[p][feat ^ which], i, feat), flat(p, i, feat))
+            for p in (1, 2) for i in range(per_part) for feat in (0, 1)
+        ]
+
+    def deliver(flip):
+        return [
+            (flat(p, i, feat), flat(KEPT[p][feat], i, (p // 2) ^ flip))
+            for p in range(4) for i in range(per_part) for feat in (0, 1)
+        ]
+
+    feat_swap = [(0, 1), (1, 0)]
+    halves = [list(range(half)), list(range(half, n_dp))]
+
+    far_give = lax.ppermute(proj_grads, both, fetch(1))
+    far_keep = lax.ppermute(proj_grads, both, fetch(0))
+    half_rows = lax.all_gather(
+        proj_grads, "dp", axis=0, tiled=True, axis_index_groups=halves
+    )
+    first_part = jnp.dot(proj_grads, val_grads, preferred_element_type=jnp.float32)
+    first_local = first_part + lax.ppermute(first_part, "feat", feat_swap)
+    first_half = lax.all_gather(
+        first_local, "dp", axis=0, tiled=True, axis_index_groups=halves
+    )
+
+    kept = jnp.asarray(KEPT, jnp.int32)
+    keep_part = kept[part, feat_index]
+    give_part = kept[part, 1 - feat_index]
+    is_inner = (part == 1) | (part == 2)
+
+    def near(which_part):
+        start = ((which_part % 2) * per_part + inner) * row_count
+        return lax.dynamic_slice_in_dim(half_rows, start, row_count, 0)
+
+    give_rows = jnp.where(is_inner, far_give, near(give_part))
+    given = lax.ppermute(pair_tile(give_rows, half_rows), "feat", feat_swap)
+    keep_rows = jnp.where(is_inner, far_keep, near(keep_part))
+    gram_cols = pair_tile(keep_rows, half_rows) + given
+    col_count = gram_cols.shape[1]
+    row_ids = (keep_part * per_part + inner) * row_count + jnp.arange(row_count, dtype=jnp.int32)
+    col_ids = (part // 2) * col_count + jnp.arange(col_count, dtype=jnp.int32)
+    pair_values = jnp.where(row_ids[:, None] == col_ids[None, :], 0.0, gram_cols)
+    interactions = lax.ppermute(pair_values.astype(jnp.bfloat16), both, deliver(0))
+    partial_sum = jnp.dot(pair_values, first_half, precision=lax.Precision.HIGHEST)
+    pair_sum = lax.ppermute(partial_sum, both, deliver(0)) + lax.ppermute(
+        partial_sum, both, deliver(1)
+    )
+    return (interactions, first_local - pair_weight * pair_sum)
+
+
 def solution(mesh):
+    n_dp = mesh.shape["dp"]
+    if mesh.shape["feat"] == 2 and n_dp % 4 == 0:
+        body = functools.partial(split_body, n_dp)
+    else:
+        body = general_body
     return jax.shard_map(
         body,
         mesh=mesh,

time: 463 us -> 376 us (0.81)
  waiting for transfers between devices: 402 us -> 290 us
  starting transfers between devices: 0.2 us -> 16.8 us
  matrix products: 37.8 us -> 44.3 us
    all_gather x2, waiting for transfers between devices: 318 us -> 55.8 us  [the longest x1 55.8 us: split_body(): lax.all_gather(proj_grads, 'dp', axis=0, tiled=True, axis_index_groups=ha...]
    ppermute x0 -> x7, waiting for transfers between devices: none -> 234 us  [the longest x1 169 us: split_body(): far_give = lax.ppermute(proj_grads, both, fetch(1))]
    reduce_scatter x1 -> x0, waiting for transfers between devices: 42.7 us -> none  [body(): lax.psum_scatter(block_row, 'feat', scatter_dimension=1, tiled=True)]
    psum x2 -> x0, waiting for transfers between devices: 40.8 us -> none  [the longest x1 22 us: body(): lax.psum(jnp.dot(proj_grads, val_grads, preferred_element_type=jnp.float3...]
    ppermute x0 -> x7, starting transfers between devices: none -> 16.7 us  [the longest x1 4.73 us: split_body(): given = lax.ppermute(pair_tile(give_rows, half_rows), 'feat', feat_swap)]
    dot_general x1 -> x2, matrix products: 29.3 us -> 37.2 us  [pair_tile(): lax.dot_general(left_rows, right_rows, (((1,), (1,)), ((), ())), preferre...]
  transfers between devices with their start and end apart: 5 -> 9, of which waited for: 5 -> 5; matrix products, arithmetic and copies ran while one was open for 7% -> 12% of each run, Pallas kernels for 0% -> 0%
where the time goes in v1:
time: 376 us; the launch traced here: 373 us
  waiting for transfers between devices  290 us (77%)
  matrix products  44.3 us (12%)
  between operations  18.8 us (5%)
  starting transfers between devices  16.8 us (4%)
    ppermute x1, waiting for transfers between devices, split_body(): far_give = lax.ppermute(proj_grads, both, fetch(1))  169 us
    all_gather x1, waiting for transfers between devices, split_body(): lax.all_gather(proj_grads, 'dp', axis=0, tiled=True, axis_index_groups=ha...  55.8 us
    ppermute x1, waiting for transfers between devices, split_body(): first_local = first_part + lax.ppermute(first_part, 'feat', feat_swap)  42.9 us
    dot_general x2, matrix products, pair_tile(): lax.dot_general(left_rows, right_rows, (((1,), (1,)), ((), ())), preferre...  37.2 us
    ppermute x1, waiting for transfers between devices, split_body(): lax.ppermute(partial_sum, both, deliver(0))  19 us
  transfers between devices with their start and end apart: 9, of which 5 were waited for; matrix products, arithmetic and copies ran while one was open for 12% of the time, Pallas kernels for 0%

profile of v1, /device:TPU:18, one launch (start us, length us, event | category | flops | bytes accessed | tf_op | source)
XLA Modules:
  0.0 373.0 jit_solution(7800507470783055310)
XLA Ops:
  7.2 0.0 copy-start
  7.2 0.0 copy-start.2
  7.2 0.0 all-gather.3.cloned.1.call-start
  7.2 0.7 all-gather.3.cloned.1.call-update
  7.9 0.0 all-gather.5.cloned.1.call-start
  8.0 1.3 collective-permute-start.1
  9.3 2.4 collective-permute-start
  11.7 0.0 copy-done.2
  11.7 0.6 fusion.16
  14.2 169.3 %collective-permute-done.1 = bf16[256,8192]{1,0:T(8,128)(2,1)} collective-permute-done((bf16[256,8192]{1,0:T(8,128)(2,1)}, bf16[256,8192]{1,0:T(8,128)(2,1)}, u32[]{:S(2)}, u32[]{:S(2)}) %collective-permute-start.1) | collective-permute-done | bytes 4194336 | tf_op jit(solution)/shard_map/ppermute | solution.py:69
  183.6 55.8 %all-gather.3.cloned.1.call-done = bf16[2048,8192]{1,0:T(8,128)(2,1)} async-done(((bf16[256,8192]{1,0:T(8,128)(2,1)}), bf16[2048,8192]{1,0:T(8,128)(2,1)}) %all-gather.3.cloned.1.call-update) | async-done | bytes 33554448 | tf_op jit(solution)/shard_map/all_gather | solution.py:71
  239.4 17.9 %fusion = f32[256,2048]{1,0:T(8,128)} fusion(bf16[2048,8192]{1,0:T(8,128)(2,1)} %all-gather.3.cloned.1.call-done, bf16[256,8192]{1,0:T(8,128)(2,1)} %collective-permute-done.1, s32[]{:T(128)S(6)} %select_n.65, pred[]{:T(512)S(6)} %or.3), kind=kOutput, calls=%fused_computation | convolution fusion | flops 8592031744 | bytes 44040196 | tf_op jit(solution)/shard_map/dot_general | solution.py:10
  257.3 4.7 %collective-permute-start.2 = (f32[256,2048]{1,0:T(8,128)}, f32[256,2048]{1,0:T(8,128)}, u32[]{:S(2)}, u32[]{:S(2)}) collective-permute-start(f32[256,2048]{1,0:T(8,128)} %fusion), channel_id=1, source_target_pairs={{0,1},{1,0},{2,3},{3,2},{4,5},{5,4},{6,7},{7,6},{8,9},{9,8},{10,11... | collective-permute-start | bytes 6291464 | tf_op jit(solution)/shard_map/ppermute | solution.py:90
  262.0 0.0 copy-done
  262.0 3.4 fusion.18
  265.4 0.1 collective-permute-start.4
  268.2 42.9 %collective-permute-done.4 = f32[256,128]{1,0:T(8,128)S(1)} collective-permute-done((f32[256,128]{1,0:T(8,128)S(1)}, f32[256,128]{1,0:T(8,128)S(1)}, u32[]{:S(2)}, u32[]{:S(2)}) %collective-permute-start.4) | collective-permute-done | bytes 131104 | tf_op jit(solution)/shard_map/ppermute | solution.py:75
  311.1 0.7 add.83
  311.7 0.0 all-gather.5.cloned.1.call-update
  311.8 0.0 copy-start.1
  311.8 0.0 collective-permute-done
  311.8 0.0 collective-permute-done.2
  311.8 19.3 %fusion.17 = (bf16[256,2048]{1,0:T(8,128)(2,1)}, f32[256,2048]{1,0:T(8,128)}) fusion(f32[256,2048]{1,0:T(8,128)} %collective-permute-done.2, bf16[2048,8192]{1,0:T(8,128)(2,1)} %all-gather.3.cloned.1.call-done, bf16[256,8192]{1,0:T(8,128)(2,1)} %collective-permute-done, s32[]{:T(128)S(6)} %select_n.61, pred[]{:T(512)S(6)} %or.3, ...), kind=kOutput, calls=%fused_computation.16 | convolution fusion | flops 8594128896 | bytes 47195140 | tf_op jit(solution)/shard_map/dot_general | solution.py:10
  331.1 4.3 %collective-permute-start.3 = (bf16[256,2048]{1,0:T(8,128)(2,1)}, bf16[256,2048]{1,0:T(8,128)(2,1)S(1)}, u32[]{:S(2)}, u32[]{:S(2)}) collective-permute-start(bf16[256,2048]{1,0:T(8,128)(2,1)} %get-tuple-element.4), channel_id=1, source_target_pairs={{0,0},{1,8},{2,2},{3,10},{4,4},{5,12},{6,6},{7,14},{8,16},{9,24},{... | collective-permute-start | bytes 3145736 | tf_op jit(solution)/shard_map/ppermute | solution.py:97
  335.4 0.0 all-gather.5.cloned.1.call-done
  335.4 3.7 fusion.19
  339.1 1.9 collective-permute-start.5
  341.0 2.1 collective-permute-start.6
  343.1 19.0 %collective-permute-done.5 = f32[256,128]{1,0:T(8,128)S(1)} collective-permute-done((f32[256,128]{1,0:T(8,128)S(1)}, f32[256,128]{1,0:T(8,128)S(1)}, u32[]{:S(2)}, u32[]{:S(2)}) %collective-permute-start.5) | collective-permute-done | bytes 131104 | tf_op jit(solution)/shard_map/ppermute | solution.py:99
  362.1 2.5 collective-permute-done.6
  364.6 0.0 copy-done.1
  364.6 0.7 multiply_subtract_fusion
  365.2 0.0 collective-permute-done.3
  365.2 1.0 copy.6
  (2 shorter events, 0.0 us)
Async XLA Ops:
  7.2 254.8 %copy-start = (bf16[8192,128]{1,0:T(8,128)(2,1)S(1)}, bf16[8192,128]{1,0:T(8,128)(2,1)}, u32[]{:S(2)}) copy-start(bf16[8192,128]{1,0:T(8,128)(2,1)} %param.4) | copy-start | bytes 6291460
  7.2 4.5 %copy-start.2 = (s32[4,2]{1,0:T(4,128)S(1)}, s32[4,2]{1,0:T(4,128)}, u32[]{:S(2)}) copy-start(s32[4,2]{1,0:T(4,128)} %constant.67.clone) | copy-start | bytes 100
  7.2 232.2 %all-gather.3.cloned.1.call-start = ((), (), s32[]{:S(2)}) async-start(), calls=%async_computation | async-start | bytes 37748736 | tf_op jit(solution)/shard_map/all_gather | solution.py:71
  7.9 327.5 %all-gather.5.cloned.1.call-start = ((), (), s32[]{:S(2)}) async-start(), calls=%async_computation.1 | async-start | bytes 1179648 | tf_op jit(solution)/shard_map/all_gather | solution.py:76
  8.0 175.6 %collective-permute-start.1 = (bf16[256,8192]{1,0:T(8,128)(2,1)}, bf16[256,8192]{1,0:T(8,128)(2,1)}, u32[]{:S(2)}, u32[]{:S(2)}) collective-permute-start(bf16[256,8192]{1,0:T(8,128)(2,1)} %param.3), channel_id=1, source_target_pairs={{24,8},{17,9},{26,10},{19,11},{28,12},{21,13},{30,14},{23,15},{0,1... | collective-permute-start | bytes 12582920 | tf_op jit(solution)/shard_map/ppermute | solution.py:69
  9.3 302.5 %collective-permute-start = (bf16[256,8192]{1,0:T(8,128)(2,1)}, bf16[256,8192]{1,0:T(8,128)(2,1)}, u32[]{:S(2)}, u32[]{:S(2)}) collective-permute-start(bf16[256,8192]{1,0:T(8,128)(2,1)} %param.3), channel_id=1, source_target_pairs={{16,8},{25,9},{18,10},{27,11},{20,12},{29,13},{22,14},{31,15},{8,1... | collective-permute-start | bytes 12582920 | tf_op jit(solution)/shard_map/ppermute | solution.py:70
  257.3 54.5 %collective-permute-start.2 = (f32[256,2048]{1,0:T(8,128)}, f32[256,2048]{1,0:T(8,128)}, u32[]{:S(2)}, u32[]{:S(2)}) collective-permute-start(f32[256,2048]{1,0:T(8,128)} %fusion), channel_id=1, source_target_pairs={{0,1},{1,0},{2,3},{3,2},{4,5},{5,4},{6,7},{7,6},{8,9},{9,8},{10,11... | collective-permute-start | bytes 6291464 | tf_op jit(solution)/shard_map/ppermute | solution.py:90
  265.4 45.7 %collective-permute-start.4 = (f32[256,128]{1,0:T(8,128)S(1)}, f32[256,128]{1,0:T(8,128)S(1)}, u32[]{:S(2)}, u32[]{:S(2)}) collective-permute-start(f32[256,128]{1,0:T(8,128)S(1)} %fusion.18), channel_id=1, source_target_pairs={{0,1},{1,0},{2,3},{3,2},{4,5},{5,4},{6,7},{7,6},{8,9},{9,8},{10,11... | collective-permute-start | bytes 393224 | tf_op jit(solution)/shard_map/ppermute | solution.py:75
  311.8 52.8 %copy-start.1 = (f32[256,128]{1,0:T(8,128)S(1)}, f32[256,128]{1,0:T(8,128)}, u32[]{:S(2)}) copy-start(f32[256,128]{1,0:T(8,128)} %add.83) | copy-start | bytes 393220
  331.1 34.1 %collective-permute-start.3 = (bf16[256,2048]{1,0:T(8,128)(2,1)}, bf16[256,2048]{1,0:T(8,128)(2,1)S(1)}, u32[]{:S(2)}, u32[]{:S(2)}) collective-permute-start(bf16[256,2048]{1,0:T(8,128)(2,1)} %get-tuple-element.4), channel_id=1, source_target_pairs={{0,0},{1,8},{2,2},{3,10},{4,4},{5,12},{6,6},{7,14},{8,16},{9,24},{... | collective-permute-start | bytes 3145736 | tf_op jit(solution)/shard_map/ppermute | solution.py:97
  339.1 23.0 %collective-permute-start.5 = (f32[256,128]{1,0:T(8,128)S(1)}, f32[256,128]{1,0:T(8,128)S(1)}, u32[]{:S(2)}, u32[]{:S(2)}) collective-permute-start(f32[256,128]{1,0:T(8,128)S(1)} %fusion.19), channel_id=1, source_target_pairs={{0,0},{1,8},{2,2},{3,10},{4,4},{5,12},{6,6},{7,14},{8,16},{9,24},{... | collective-permute-start | bytes 393224 | tf_op jit(solution)/shard_map/ppermute | solution.py:99
  341.0 23.5 %collective-permute-start.6 = (f32[256,128]{1,0:T(8,128)S(1)}, f32[256,128]{1,0:T(8,128)S(1)}, u32[]{:S(2)}, u32[]{:S(2)}) collective-permute-start(f32[256,128]{1,0:T(8,128)S(1)} %fusion.19), channel_id=1, source_target_pairs={{0,1},{1,9},{2,3},{3,11},{4,5},{5,13},{6,7},{7,15},{8,17},{9,25},{... | collective-permute-start | bytes 393224 | tf_op jit(solution)/shard_map/ppermute | solution.py:99
Sparse Core Ops, SparseCore 0:
  9.6 229.6 all-gather.2
  311.9 19.6 all-gather.4

commit v2 on v0

--- a/solution.py
+++ b/solution.py
@@ -10,7 +10,7 @@
     )
 
 
-def body(proj_grads, val_grads):
+def general_body(proj_grads, val_grads):
     row_count = proj_grads.shape[0]
     pair_weight = 1.0 / row_count**0.5
     dp_index = lax.axis_index("dp")
@@ -32,9 +32,119 @@
     return (pair_values.astype(jnp.bfloat16), data_scores)
 
 
+ROWS_OF = ((0, 1), (2, 3), (1, 0), (3, 2))
+
+
+def split_body(proj_grads, val_grads):
+    row_count, width = proj_grads.shape
+    pair_weight = 1.0 / row_count**0.5
+    dp_index = lax.axis_index("dp")
+    feat_index = lax.axis_index("feat")
+    part, side, core = dp_index // 4, dp_index // 2 % 2, dp_index % 2
+    is_inner = (part == 1) | (part == 2)
+    both = ("dp", "feat")
+
+    def at(part, side, core):
+        return (part * 2 + side) * 2 + core
+
+    def moves(to, parts=range(4)):
+        return [
+            (at(p, s, c), at(*to(p, s, c))) for p in parts for s in (0, 1) for c in (0, 1)
+        ]
+
+    core_swap = moves(lambda p, s, c: (p, s, 1 - c))
+    side_swap = moves(lambda p, s, c: (p, 1 - s, c))
+    part_swap = moves(lambda p, s, c: (p ^ 1, s, c))
+    near_swap = moves(lambda p, s, c: (3 - p, s, c), (1, 2))
+    far_move = moves(lambda p, s, c: (2 if p == 0 else 1, s, c), (0, 3))
+    feat_swap = [(0, 1), (1, 0)]
+
+    def ordered(flag, mine, other, axis):
+        low = jnp.where(flag == 0, mine, other)
+        high = jnp.where(flag == 0, other, mine)
+        return jnp.concatenate([low, high], axis)
+
+    half_width = width // 2
+    mine = lax.dynamic_slice_in_dim(proj_grads, core * half_width, half_width, 1)
+    give = lax.dynamic_slice_in_dim(proj_grads, (1 - core) * half_width, half_width, 1)
+    own = ordered(core, mine, lax.ppermute(give, "dp", core_swap), 0)
+
+    by_part = lax.ppermute(own, "dp", part_swap)
+    by_side = lax.ppermute(own, "dp", side_swap)
+    near = lax.ppermute(own, "dp", near_swap)
+    first_part = jnp.dot(proj_grads, val_grads, preferred_element_type=jnp.float32)
+    first_local = first_part + lax.ppermute(first_part, "feat", feat_swap)
+
+    own_late, by_part_late, first_local = lax.optimization_barrier((own, by_part, first_local))
+    far = lax.ppermute(own_late, "dp", far_move)
+    by_both = lax.ppermute(by_part_late, "dp", side_swap)
+    half = lax.axis_size("dp") // 2
+    first_half = lax.all_gather(
+        first_local, "dp", axis=0, tiled=True,
+        axis_index_groups=[list(range(half)), list(range(half, 2 * half))],
+    )
+
+    def summed(tile):
+        rows = tile.shape[0] // 2
+        keep = lax.dynamic_slice_in_dim(tile, core * rows, rows, 0)
+        send = lax.dynamic_slice_in_dim(tile, (1 - core) * rows, rows, 0)
+        tile = keep + lax.ppermute(send, "dp", core_swap)
+        rows = rows // 2
+        keep = lax.dynamic_slice_in_dim(tile, feat_index * rows, rows, 0)
+        send = lax.dynamic_slice_in_dim(tile, (1 - feat_index) * rows, rows, 0)
+        return keep + lax.ppermute(send, "feat", feat_swap)
+
+    rows_a = jnp.where(is_inner, near, own)
+    early = summed(
+        jnp.concatenate([pair_tile(rows_a, cols) for cols in (own, by_side, by_part)], 1)
+    )
+    far, by_both, early, first_half = lax.optimization_barrier((far, by_both, early, first_half))
+    rows_b = jnp.where(is_inner, far, by_part)
+    late_b = summed(
+        jnp.concatenate([pair_tile(rows_b, cols) for cols in (own, by_side, by_part, by_both)], 1)
+    )
+    late_a = summed(pair_tile(rows_a, by_both))
+    gram = jnp.concatenate([jnp.concatenate([early, late_a], 1), late_b], 0)
+
+    chip_cols = own.shape[0]
+    own_x, side_x, part_x, both_x = (
+        gram[:, i * chip_cols:(i + 1) * chip_cols] for i in range(4)
+    )
+    gram_cols = ordered(
+        part % 2,
+        ordered(side, own_x, side_x, 1),
+        ordered(side, part_x, both_x, 1),
+        1,
+    )
+    rows_of = jnp.asarray(ROWS_OF, jnp.int32)[part]
+    piece = row_count // 2
+    row_base = ((rows_of * 2 + side) * 2 + core) * row_count + feat_index * piece
+    row_ids = (row_base[:, None] + jnp.arange(piece, dtype=jnp.int32)[None, :]).reshape(-1)
+    col_count = gram_cols.shape[1]
+    col_ids = (part // 2) * col_count + jnp.arange(col_count, dtype=jnp.int32)
+    pair_values = jnp.where(row_ids[:, None] == col_ids[None, :], 0.0, gram_cols)
+    partial_sum = jnp.dot(pair_values, first_half, precision=lax.Precision.HIGHEST)
+
+    def deliver(values):
+        out = []
+        for flip in (0, 1):
+            sent = jnp.where((feat_index ^ flip) == 0, values[:piece], values[piece:])
+            out.append(lax.ppermute(sent, both, [
+                (at(p, s, c) * 2 + f, at(ROWS_OF[p][f ^ flip], s, c) * 2 + p // 2)
+                for p in range(4) for s in (0, 1) for c in (0, 1) for f in (0, 1)
+            ]))
+        return ordered((part + feat_index) % 2, out[0], out[1], 0)
+
+    half_sum = deliver(partial_sum)
+    interactions = deliver(pair_values.astype(jnp.bfloat16))
+    pair_sum = half_sum + lax.ppermute(half_sum, "feat", feat_swap)
+    return (interactions, first_local - pair_weight * pair_sum)
+
+
 def solution(mesh):
+    split = mesh.shape["feat"] == 2 and mesh.shape["dp"] == 16
     return jax.shard_map(
-        body,
+        split_body if split else general_body,
         mesh=mesh,
         in_specs=(P("dp", "feat"), P("feat", None)),
         out_specs=(P("dp", "feat"), P("dp", None)),

time: 463 us -> 331 us (0.71)
  waiting for transfers between devices: 402 us -> 206 us
  starting transfers between devices: 0.2 us -> 29.4 us
  other arithmetic: 4.42 us -> 25.8 us
  local copies, waits for them, and re-layouts: 1.55 us -> 14.6 us
    all_gather x2 -> x1, waiting for transfers between devices: 318 us -> 0.02 us  [split_body(): lax.all_gather(first_local, 'dp', axis=0, tiled=True, axis_index_groups=[...]
    ppermute x0 -> x18, waiting for transfers between devices: none -> 206 us  [the longest x1 81.9 us: split_body(): by_part = lax.ppermute(own, 'dp', part_swap)]
    reduce_scatter x1 -> x0, waiting for transfers between devices: 42.7 us -> none  [body(): lax.psum_scatter(block_row, 'feat', scatter_dimension=1, tiled=True)]
    psum x2 -> x0, waiting for transfers between devices: 40.8 us -> none  [the longest x1 22 us: body(): lax.psum(jnp.dot(proj_grads, val_grads, preferred_element_type=jnp.float3...]
    ppermute x0 -> x18, starting transfers between devices: none -> 29.3 us  [the longest x4 16 us: deliver(): lax.ppermute(sent, both, [(at(p, s, c) * 2 + f, at(ROWS_OF[p][f ^ flip],...]
    select_n x0 -> x9, other arithmetic: none -> 10.9 us  [the longest x1 4.39 us: split_body(): rows_a = jnp.where(is_inner, near, own)]
    add x2 -> x10, other arithmetic: 0.01 us -> 9.49 us  [the longest x3 4.28 us: summed(): tile = keep + lax.ppermute(send, 'dp', core_swap)]
    dynamic_slice x0 -> x7, local copies, waits for them, and re-layouts: none -> 6.78 us  [the longest x1 3.32 us: split_body(): lax.dynamic_slice_in_dim(proj_grads, (1 - core) * half_width, half_width, 1)]
  transfers between devices with their start and end apart: 5 -> 19, of which waited for: 5 -> 10; matrix products, arithmetic and copies ran while one was open for 7% -> 11% of each run, Pallas kernels for 0% -> 0%
where the time goes in v2:
time: 331 us
  waiting for transfers between devices  206 us (62%)
  matrix products  40 us (12%)
  starting transfers between devices  29.4 us (9%)
  other arithmetic  25.8 us (8%)
  local copies, waits for them, and re-layouts  14.6 us (4%)
  between operations  14.6 us (4%)
    ppermute x1, waiting for transfers between devices, split_body(): by_part = lax.ppermute(own, 'dp', part_swap)  81.9 us
    ppermute x1, waiting for transfers between devices, split_body(): far = lax.ppermute(own_late, 'dp', far_move)  47.8 us
    ppermute x3, waiting for transfers between devices, summed(): return keep + lax.ppermute(send, 'feat', feat_swap)  45.5 us
    dot_general x8, matrix products, pair_tile(): lax.dot_general(left_rows, right_rows, (((1,), (1,)), ((), ())), preferre...  34.9 us
    ppermute x4, starting transfers between devices, deliver(): lax.ppermute(sent, both, [(at(p, s, c) * 2 + f, at(ROWS_OF[p][f ^ flip],...  16 us
    ppermute x1, waiting for transfers between devices, split_body(): pair_sum = half_sum + lax.ppermute(half_sum, 'feat', feat_swap)  9.39 us
    ppermute x4, waiting for transfers between devices, deliver(): lax.ppermute(sent, both, [(at(p, s, c) * 2 + f, at(ROWS_OF[p][f ^ flip],...  8.87 us
    unnamed x31, local copies, waits for them, and re-layouts  7.8 us
  transfers between devices with their start and end apart: 19, of which 10 were waited for; matrix products, arithmetic and copies ran while one was open for 11% of the time, Pallas kernels for 0%

profile of v2, /device:TPU:18, one launch (start us, length us, event | category | flops | bytes accessed | tf_op | source)
XLA Modules:
  0.0 330.7 jit_solution(7517110170224833456)
XLA Ops:
  7.2 3.3 %constant_dynamic-slice_fusion.6 = bf16[256,4096]{1,0:T(8,128)(2,1)} fusion(bf16[256,8192]{1,0:T(8,128)(2,1)} %param.3, s32[]{:T(128)S(6)} %select_n.182), kind=kLoop, calls=%fused_computation.46 | loop fusion | bytes 4194308 | tf_op jit(solution)/shard_map/dynamic_slice | solution.py:69
  10.6 4.5 %collective-permute-done = bf16[256,4096]{1,0:T(8,128)(2,1)} collective-permute-done((bf16[256,4096]{1,0:T(8,128)(2,1)}, bf16[256,4096]{1,0:T(8,128)(2,1)}, u32[]{:S(2)}, u32[]{:S(2)}) %collective-permute-start) | collective-permute-done | bytes 2097184 | tf_op jit(solution)/shard_map/ppermute | solution.py:70
  15.1 3.4 %broadcast_select_fusion.3 = (bf16[256,4096]{1,0:T(8,128)(2,1)S(1)}, bf16[256,4096]{1,0:T(8,128)(2,1)S(1)}) fusion(bf16[256,4096]{1,0:T(8,128)(2,1)} %collective-permute-done, pred[]{:T(512)S(6)} %eq.60, bf16[256,8192]{1,0:T(8,128)(2,1)} %param.3, s32[]{:T(128)S(6)} %select_n.181), kind=kLoop, calls=%fused_computation.9 | loop fusion | flops 2097152 | bytes 8388613 | tf_op jit(solution)/shard_map/jit(_where)/select_n | solution.py:63
  18.5 2.5 pad_maximum_fusion
  21.0 0.5 copy-done.2
  21.5 1.1 copy-done.4
  22.6 1.6 collective-permute-start.1
  24.1 1.9 collective-permute-start.5
  26.1 0.6 collective-permute-start.6
  26.7 1.2 fusion.18
  27.9 1.6 collective-permute-start.2
  29.5 3.5 %collective-permute-done.2 = f32[256,128]{1,0:T(8,128)S(1)} collective-permute-done((f32[256,128]{1,0:T(8,128)S(1)}, f32[256,128]{1,0:T(8,128)S(1)}, u32[]{:S(2)}, u32[]{:S(2)}) %collective-permute-start.2) | collective-permute-done | bytes 131104 | tf_op jit(solution)/shard_map/ppermute | solution.py:76
  33.0 0.7 add.159
  33.6 81.9 %collective-permute-done.1 = bf16[512,4096]{1,0:T(8,128)(2,1)} collective-permute-done((bf16[512,4096]{1,0:T(8,128)(2,1)}, bf16[512,4096]{1,0:T(8,128)(2,1)}, u32[]{:S(2)}, u32[]{:S(2)}) %collective-permute-start.1) | collective-permute-done | bytes 4194336 | tf_op jit(solution)/shard_map/ppermute | solution.py:72
  115.5 1.3 collective-permute-start.3
  116.8 0.6 collective-permute-start.4
  117.4 1.3 collective-permute-done.5
  118.7 4.4 %broadcast_select_fusion.1 = bf16[512,4096]{1,0:T(8,128)(2,1)S(1)} fusion(bf16[512,4096]{1,0:T(8,128)(2,1)} %collective-permute-done.5, pred[]{:T(512)S(6)} %or.3, bf16[256,4096]{1,0:T(8,128)(2,1)} %copy-done.4, bf16[256,4096]{1,0:T(8,128)(2,1)} %copy-done.2), kind=kLoop, calls=%fused_computation.3 | loop fusion | flops 10485760 | bytes 12582913 | tf_op jit(solution)/shard_map/jit(_where)/select_n | solution.py:97
  123.1 2.5 fusion.17
  125.6 4.7 %fusion.20 = f32[512,512]{0,1:T(8,128)S(1)} fusion(bf16[512,4096]{1,0:T(8,128)(2,1)S(1)} %broadcast_select_fusion.1, bf16[512,4096]{1,0:T(8,128)(2,1)} %collective-permute-done.1), kind=kOutput, calls=%fused_computation.62 | convolution fusion | flops 2147483648 | bytes 9437184 | tf_op jit(solution)/shard_map/dot_general | solution.py:8
  130.4 4.7 %fusion.19 = f32[512,512]{0,1:T(8,128)S(1)} fusion(bf16[512,4096]{1,0:T(8,128)(2,1)S(1)} %broadcast_select_fusion.1, bf16[512,4096]{1,0:T(8,128)(2,1)} %collective-permute-done.6), kind=kOutput, calls=%fused_computation.61 | convolution fusion | flops 2147483648 | bytes 9437184 | tf_op jit(solution)/shard_map/dot_general | solution.py:8
  135.2 0.4 pad_maximum_fusion.2
  135.6 1.6 copy-done.10
  137.2 1.3 constant_dynamic-slice_fusion.5
  138.6 3.7 %collective-permute-done.7 = f32[256,1536]{0,1:T(8,128)} collective-permute-done((f32[256,1536]{0,1:T(8,128)}, f32[256,1536]{0,1:T(8,128)}, u32[]{:S(2)}, u32[]{:S(2)}) %collective-permute-start.7) | collective-permute-done | bytes 1572896 | tf_op jit(solution)/shard_map/ppermute | solution.py:91
  142.3 2.1 dynamic-slice_add_fusion.1
  144.4 1.1 copy-done.11
  145.6 1.6 collective-permute-start.8
  147.2 18.2 %collective-permute-done.8 = f32[128,1536]{0,1:T(8,128)} collective-permute-done((f32[128,1536]{0,1:T(8,128)S(1)}, f32[128,1536]{0,1:T(8,128)}, u32[]{:S(2)}, u32[]{:S(2)}) %collective-permute-start.8) | collective-permute-done | bytes 786464 | tf_op jit(solution)/shard_map/ppermute | solution.py:95
  165.3 1.5 dynamic-slice_add_fusion.3
  166.8 47.8 %collective-permute-done.3 = bf16[512,4096]{1,0:T(8,128)(2,1)} collective-permute-done((bf16[512,4096]{1,0:T(8,128)(2,1)}, bf16[512,4096]{1,0:T(8,128)(2,1)}, u32[]{:S(2)}, u32[]{:S(2)}) %collective-permute-start.3) | collective-permute-done | bytes 4194336 | tf_op jit(solution)/shard_map/ppermute | solution.py:79
  214.6 2.6 broadcast_select_fusion
  217.2 2.5 fusion.16
  219.8 4.7 %fusion.24 = f32[512,512]{0,1:T(8,128)S(1)} fusion(bf16[512,4096]{1,0:T(8,128)(2,1)S(1)} %broadcast_select_fusion, bf16[512,4096]{1,0:T(8,128)(2,1)} %collective-permute-done.4), kind=kOutput, calls=%fused_computation.66 | convolution fusion | flops 2147483648 | bytes 9437184 | tf_op jit(solution)/shard_map/dot_general | solution.py:8
  224.5 5.0 %fusion.22 = f32[512,512]{0,1:T(8,128)S(1)} fusion(bf16[512,4096]{1,0:T(8,128)(2,1)S(1)} %broadcast_select_fusion, bf16[512,4096]{1,0:T(8,128)(2,1)} %collective-permute-done.6), kind=kOutput, calls=%fused_computation.64 | convolution fusion | flops 2147483648 | bytes 9437184 | tf_op jit(solution)/shard_map/dot_general | solution.py:8
  229.5 4.7 %fusion.23 = f32[512,512]{0,1:T(8,128)S(1)} fusion(bf16[512,4096]{1,0:T(8,128)(2,1)S(1)} %broadcast_select_fusion, bf16[512,4096]{1,0:T(8,128)(2,1)} %collective-permute-done.1), kind=kOutput, calls=%fused_computation.65 | convolution fusion | flops 2147483648 | bytes 9437184 | tf_op jit(solution)/shard_map/dot_general | solution.py:8
  234.2 0.5 pad_maximum_fusion.1
  234.8 2.0 copy-done.8
  236.8 0.2 constant_dynamic-slice_fusion.1
  237.2 6.0 %fusion.21 = f32[512,512]{0,1:T(8,128)S(1)} fusion(bf16[512,4096]{1,0:T(8,128)(2,1)} %copy-done.12, bf16[512,4096]{1,0:T(8,128)(2,1)} %collective-permute-done.4), kind=kOutput, calls=%fused_computation.63 | convolution fusion | flops 2147483648 | bytes 9437184 | tf_op jit(solution)/shard_map/dot_general | solution.py:8
  243.2 0.5 collective-permute-start.9
  243.7 2.1 dynamic-slice_add_fusion
  245.8 1.0 constant_dynamic-slice_fusion
  246.9 1.5 collective-permute-start.12
  248.5 0.7 constant_dynamic-slice_fusion.2
  249.2 0.5 collective-permute-start.10
  249.7 0.7 fusion.13
  250.5 27.3 %collective-permute-done.10 = f32[128,512]{0,1:T(8,128)} collective-permute-done((f32[128,512]{0,1:T(8,128)}, f32[128,512]{0,1:T(8,128)}, u32[]{:S(2)}, u32[]{:S(2)}) %collective-permute-start.10) | collective-permute-done | bytes 262176 | tf_op jit(solution)/shard_map/ppermute | solution.py:95
  277.8 1.0 dynamic-slice_add_fusion.5
  278.8 1.3 dynamic-slice_add_fusion.2
  280.1 0.1 pad_maximum_fusion.3
  280.3 0.2 slice_select_fusion.3
  280.5 0.1 fusion.6
  280.6 1.0 fusion.1
  281.7 3.8 %fusion = f32[256,128]{1,0:T(8,128)S(1)} fusion(f32[2048,128]{1,0:T(8,128)S(1)} %copy-done.14, f32[256,1024]{0,1:T(8,128)S(1)} %get-tuple-element.21, f32[256,1024]{0,1:T(8,128)S(1)} %get-tuple-element.20, s32[256]{0:T(256)S(1)} %add_bitcast_fusion, s32[2048]{0:T(1024)S(1)} %iota_add_fusion), kind=kOutput, calls=%fused_computation.11 | convolution fusion | flops 806879232 | bytes 3286016 | tf_op jit(solution)/shard_map/dot_general | solution.py:126
  285.5 3.4 %collective-permute-start.15 = (f32[128,128]{1,0:T(8,128)S(1)}, f32[128,128]{1,0:T(8,128)S(1)}, u32[]{:S(2)}, u32[]{:S(2)}) collective-permute-start(f32[128,128]{1,0:T(8,128)S(1)} %get-tuple-element.32), channel_id=1, source_target_pairs={{0,0},{1,8},{2,2},{3,10},{4,4},{5,12},{6,6},{7,14},{8,16},{9,24},{... | collective-permute-start | bytes 196616 | tf_op jit(solution)/shard_map/ppermute | solution.py:132
  288.9 5.3 %collective-permute-start.16 = (f32[128,128]{1,0:T(8,128)S(1)}, f32[128,128]{1,0:T(8,128)S(1)}, u32[]{:S(2)}, u32[]{:S(2)}) collective-permute-start(f32[128,128]{1,0:T(8,128)S(1)} %get-tuple-element.33), channel_id=1, source_target_pairs={{0,8},{1,0},{2,10},{3,2},{4,12},{5,4},{6,14},{7,6},{8,24},{9,16},{... | collective-permute-start | bytes 196616 | tf_op jit(solution)/shard_map/ppermute | solution.py:132
  294.3 2.4 collective-permute-start.13
  296.6 4.9 %collective-permute-start.14 = (bf16[128,2048]{0,1:T(8,128)(2,1)S(1)}, bf16[128,2048]{0,1:T(8,128)(2,1)S(1)}, u32[]{:S(2)}, u32[]{:S(2)}) collective-permute-start(bf16[128,2048]{0,1:T(8,128)(2,1)S(1)} %get-tuple-element.29), channel_id=1, source_target_pairs={{0,8},{1,0},{2,10},{3,2},{4,12},{5,4},{6,14},{7,6},{8,24},{9,16},{... | collective-permute-start | bytes 1572872 | tf_op jit(solution)/shard_map/ppermute | solution.py:132
  301.6 1.6 collective-permute-start.17
  303.3 9.4 %collective-permute-done.17 = f32[256,128]{1,0:T(8,128)S(1)} collective-permute-done((f32[256,128]{1,0:T(8,128)S(1)}, f32[256,128]{1,0:T(8,128)S(1)}, u32[]{:S(2)}, u32[]{:S(2)}) %collective-permute-start.17) | collective-permute-done | bytes 131104 | tf_op jit(solution)/shard_map/ppermute | solution.py:140
  312.7 0.7 multiply_subtract_fusion
  313.4 8.9 %collective-permute-done.14 = bf16[128,2048]{0,1:T(8,128)(2,1)S(1)} collective-permute-done((bf16[128,2048]{0,1:T(8,128)(2,1)S(1)}, bf16[128,2048]{0,1:T(8,128)(2,1)S(1)}, u32[]{:S(2)}, u32[]{:S(2)}) %collective-permute-start.14) | collective-permute-done | bytes 524320 | tf_op jit(solution)/shard_map/ppermute | solution.py:132
  322.4 1.4 copy.5
  (50 shorter events, 0.8 us)
Async XLA Ops:
  7.2 19.5 %copy-start = (bf16[8192,128]{1,0:T(8,128)(2,1)S(1)}, bf16[8192,128]{1,0:T(8,128)(2,1)}, u32[]{:S(2)}) copy-start(bf16[8192,128]{1,0:T(8,128)(2,1)} %param.4) | copy-start | bytes 6291460
  7.2 159.6 %all-gather.2.cloned.1.call-start = ((), (), s32[]{:S(2)}) async-start(), calls=%async_computation | async-start | bytes 1179648 | tf_op jit(solution)/shard_map/all_gather | solution.py:82
  10.6 4.5 %collective-permute-start = (bf16[256,4096]{1,0:T(8,128)(2,1)}, bf16[256,4096]{1,0:T(8,128)(2,1)}, u32[]{:S(2)}, u32[]{:S(2)}) collective-permute-start(bf16[256,4096]{1,0:T(8,128)(2,1)} %constant_dynamic-slice_fusion.6), channel_id=1, source_target_pairs={{0,2},{2,0},{4,6},{6,4},{8,10},{10,8},{12,14},{14,12},{16,18},{18,... | collective-permute-start | bytes 6291464 | tf_op jit(solution)/shard_map/ppermute | solution.py:70
  18.4 3.1 copy-start.2
  18.5 4.1 %copy-start.4 = (bf16[256,4096]{1,0:T(8,128)(2,1)}, bf16[256,4096]{1,0:T(8,128)(2,1)S(1)}, u32[]{:S(2)}) copy-start(bf16[256,4096]{1,0:T(8,128)(2,1)S(1)} %get-tuple-element.19) | copy-start | bytes 6291460
  18.5 8.2 %copy-start.7 = (bf16[256,8192]{1,0:T(8,128)(2,1)S(1)}, bf16[256,8192]{1,0:T(8,128)(2,1)}, u32[]{:S(2)}) copy-start(bf16[256,8192]{1,0:T(8,128)(2,1)} %param.3) | copy-start | bytes 12582916
  22.6 92.9 %collective-permute-start.1 = (bf16[512,4096]{1,0:T(8,128)(2,1)}, bf16[512,4096]{1,0:T(8,128)(2,1)}, u32[]{:S(2)}, u32[]{:S(2)}) collective-permute-start(bf16[512,4096]{1,0:T(8,128)(2,1)} %pad_maximum_fusion), channel_id=1, source_target_pairs={{0,8},{2,10},{4,12},{6,14},{8,0},{10,2},{12,4},{14,6},{16,24},{18,... | collective-permute-start | bytes 12582920 | tf_op jit(solution)/shard_map/ppermute | solution.py:72
  24.1 94.5 %collective-permute-start.5 = (bf16[512,4096]{1,0:T(8,128)(2,1)}, bf16[512,4096]{1,0:T(8,128)(2,1)}, u32[]{:S(2)}, u32[]{:S(2)}) collective-permute-start(bf16[512,4096]{1,0:T(8,128)(2,1)} %pad_maximum_fusion), channel_id=1, source_target_pairs={{8,16},{10,18},{12,20},{14,22},{16,8},{18,10},{20,12},{22,14},{9,1... | collective-permute-start | bytes 12582920 | tf_op jit(solution)/shard_map/ppermute | solution.py:74
  26.1 104.3 %collective-permute-start.6 = (bf16[512,4096]{1,0:T(8,128)(2,1)}, bf16[512,4096]{1,0:T(8,128)(2,1)}, u32[]{:S(2)}, u32[]{:S(2)}) collective-permute-start(bf16[512,4096]{1,0:T(8,128)(2,1)} %pad_maximum_fusion), channel_id=1, source_target_pairs={{0,4},{2,6},{4,0},{6,2},{8,12},{10,14},{12,8},{14,10},{16,20},{18,... | collective-permute-start | bytes 12582920 | tf_op jit(solution)/shard_map/ppermute | solution.py:73
  27.9 5.0 %collective-permute-start.2 = (f32[256,128]{1,0:T(8,128)S(1)}, f32[256,128]{1,0:T(8,128)S(1)}, u32[]{:S(2)}, u32[]{:S(2)}) collective-permute-start(f32[256,128]{1,0:T(8,128)S(1)} %fusion.18), channel_id=1, source_target_pairs={{0,1},{1,0},{2,3},{3,2},{4,5},{5,4},{6,7},{7,6},{8,9},{9,8},{10,11... | collective-permute-start | bytes 393224 | tf_op jit(solution)/shard_map/ppermute | solution.py:76
  33.6 89.4 %copy-start.3 = (bf16[256,4096]{1,0:T(8,128)(2,1)S(1)}, bf16[256,4096]{1,0:T(8,128)(2,1)}, u32[]{:S(2)}) copy-start(bf16[256,4096]{1,0:T(8,128)(2,1)} %copy-done.2) | copy-start | bytes 6291460
  33.6 89.5 %copy-start.5 = (bf16[256,4096]{1,0:T(8,128)(2,1)S(1)}, bf16[256,4096]{1,0:T(8,128)(2,1)}, u32[]{:S(2)}) copy-start(bf16[256,4096]{1,0:T(8,128)(2,1)} %copy-done.4) | copy-start | bytes 6291460
  115.5 99.1 %collective-permute-start.3 = (bf16[512,4096]{1,0:T(8,128)(2,1)}, bf16[512,4096]{1,0:T(8,128)(2,1)}, u32[]{:S(2)}, u32[]{:S(2)}) collective-permute-start(bf16[512,4096]{1,0:T(8,128)(2,1)} %pad_maximum_fusion), channel_id=1, source_target_pairs={{0,16},{2,18},{4,20},{6,22},{24,8},{26,10},{28,12},{30,14},{1,17},... | collective-permute-start | bytes 12582920 | tf_op jit(solution)/shard_map/ppermute | solution.py:79
  116.8 97.8 %collective-permute-start.4 = (bf16[512,4096]{1,0:T(8,128)(2,1)}, bf16[512,4096]{1,0:T(8,128)(2,1)}, u32[]{:S(2)}, u32[]{:S(2)}) collective-permute-start(bf16[512,4096]{1,0:T(8,128)(2,1)} %collective-permute-done.1), channel_id=1, source_target_pairs={{0,4},{2,6},{4,0},{6,2},{8,12},{10,14},{12,8},{14,10},{16,20},{18,... | collective-permute-start | bytes 12582920 | tf_op jit(solution)/shard_map/ppermute | solution.py:80
  123.1 7.3 %copy-start.12 = (bf16[512,4096]{1,0:T(8,128)(2,1)}, bf16[512,4096]{1,0:T(8,128)(2,1)S(1)}, u32[]{:S(2)}) copy-start(bf16[512,4096]{1,0:T(8,128)(2,1)S(1)} %broadcast_select_fusion.1) | copy-start | bytes 12582916
  135.6 1.6 copy-start.10
  138.5 3.8 %collective-permute-start.7 = (f32[256,1536]{0,1:T(8,128)}, f32[256,1536]{0,1:T(8,128)}, u32[]{:S(2)}, u32[]{:S(2)}) collective-permute-start(f32[256,1536]{0,1:T(8,128)} %constant_dynamic-slice_fusion.5), channel_id=1, source_target_pairs={{0,2},{2,0},{4,6},{6,4},{8,10},{10,8},{12,14},{14,12},{16,18},{18,... | collective-permute-start | bytes 4718600 | tf_op jit(solution)/shard_map/ppermute | solution.py:91
  144.4 1.1 copy-start.11
  145.6 19.8 %collective-permute-start.8 = (f32[128,1536]{0,1:T(8,128)S(1)}, f32[128,1536]{0,1:T(8,128)}, u32[]{:S(2)}, u32[]{:S(2)}) collective-permute-start(f32[128,1536]{0,1:T(8,128)S(1)} %constant_dynamic-slice_fusion.4), channel_id=1, source_target_pairs={{0,1},{1,0},{2,3},{3,2},{4,5},{5,4},{6,7},{7,6},{8,9},{9,8},{10,11... | collective-permute-start | bytes 2359304 | tf_op jit(solution)/shard_map/ppermute | solution.py:95
  166.8 50.4 %copy-start.6 = (bf16[256,4096]{1,0:T(8,128)(2,1)S(1)}, bf16[256,4096]{1,0:T(8,128)(2,1)}, u32[]{:S(2)}) copy-start(bf16[256,4096]{1,0:T(8,128)(2,1)} %copy-done.4) | copy-start | bytes 6291460
  234.8 2.0 copy-start.8
  237.0 6.7 %collective-permute-start.11 = (f32[256,2048]{0,1:T(8,128)S(1)}, f32[256,2048]{0,1:T(8,128)}, u32[]{:S(2)}, u32[]{:S(2)}) collective-permute-start(f32[256,2048]{0,1:T(8,128)S(1)} %constant_dynamic-slice_fusion.1), channel_id=1, source_target_pairs={{0,2},{2,0},{4,6},{6,4},{8,10},{10,8},{12,14},{14,12},{16,18},{18,... | collective-permute-start | bytes 6291464 | tf_op jit(solution)/shard_map/ppermute | solution.py:91
  237.2 6.5 %copy-start.9 = (f32[512,2048]{0,1:T(8,128)S(1)}, f32[512,2048]{0,1:T(8,128)}, u32[]{:S(2)}) copy-start(f32[512,2048]{0,1:T(8,128)} %copy-done.8) | copy-start | bytes 12582916
  243.2 5.2 %collective-permute-start.9 = (f32[256,512]{0,1:T(8,128)S(1)}, f32[256,512]{0,1:T(8,128)S(1)}, u32[]{:S(2)}, u32[]{:S(2)}) collective-permute-start(f32[256,512]{0,1:T(8,128)S(1)} %constant_dynamic-slice_fusion.3), channel_id=1, source_target_pairs={{0,2},{2,0},{4,6},{6,4},{8,10},{10,8},{12,14},{14,12},{16,18},{18,... | collective-permute-start | bytes 1572872 | tf_op jit(solution)/shard_map/ppermute | solution.py:91
  246.9 31.9 %collective-permute-start.12 = (f32[128,2048]{0,1:T(8,128)}, f32[128,2048]{0,1:T(8,128)}, u32[]{:S(2)}, u32[]{:S(2)}) collective-permute-start(f32[128,2048]{0,1:T(8,128)} %constant_dynamic-slice_fusion), channel_id=1, source_target_pairs={{0,1},{1,0},{2,3},{3,2},{4,5},{5,4},{6,7},{7,6},{8,9},{9,8},{10,11... | collective-permute-start | bytes 3145736 | tf_op jit(solution)/shard_map/ppermute | solution.py:95
  249.2 28.6 %collective-permute-start.10 = (f32[128,512]{0,1:T(8,128)}, f32[128,512]{0,1:T(8,128)}, u32[]{:S(2)}, u32[]{:S(2)}) collective-permute-start(f32[128,512]{0,1:T(8,128)} %constant_dynamic-slice_fusion.2), channel_id=1, source_target_pairs={{0,1},{1,0},{2,3},{3,2},{4,5},{5,4},{6,7},{7,6},{8,9},{9,8},{10,11... | collective-permute-start | bytes 786440 | tf_op jit(solution)/shard_map/ppermute | solution.py:95
  280.5 1.2 copy-start.14
  280.6 32.0 %copy-start.13 = (f32[256,128]{1,0:T(8,128)S(1)}, f32[256,128]{1,0:T(8,128)}, u32[]{:S(2)}) copy-start(f32[256,128]{1,0:T(8,128)} %add.159) | copy-start | bytes 393220
  285.5 16.1 %collective-permute-start.15 = (f32[128,128]{1,0:T(8,128)S(1)}, f32[128,128]{1,0:T(8,128)S(1)}, u32[]{:S(2)}, u32[]{:S(2)}) collective-permute-start(f32[128,128]{1,0:T(8,128)S(1)} %get-tuple-element.32), channel_id=1, source_target_pairs={{0,0},{1,8},{2,2},{3,10},{4,4},{5,12},{6,6},{7,14},{8,16},{9,24},{... | collective-permute-start | bytes 196616 | tf_op jit(solution)/shard_map/ppermute | solution.py:132
  288.9 12.7 %collective-permute-start.16 = (f32[128,128]{1,0:T(8,128)S(1)}, f32[128,128]{1,0:T(8,128)S(1)}, u32[]{:S(2)}, u32[]{:S(2)}) collective-permute-start(f32[128,128]{1,0:T(8,128)S(1)} %get-tuple-element.33), channel_id=1, source_target_pairs={{0,8},{1,0},{2,10},{3,2},{4,12},{5,4},{6,14},{7,6},{8,24},{9,16},{... | collective-permute-start | bytes 196616 | tf_op jit(solution)/shard_map/ppermute | solution.py:132
  294.2 29.7 %copy-start.1 = (bf16[8192,128]{1,0:T(8,128)(2,1)S(1)}, bf16[8192,128]{1,0:T(8,128)(2,1)}, u32[]{:S(2)}) copy-start(bf16[8192,128]{1,0:T(8,128)(2,1)} %param.4) | copy-start | bytes 6291460
  294.3 19.1 %collective-permute-start.13 = (bf16[128,2048]{0,1:T(8,128)(2,1)S(1)}, bf16[128,2048]{0,1:T(8,128)(2,1)S(1)}, u32[]{:S(2)}, u32[]{:S(2)}) collective-permute-start(bf16[128,2048]{0,1:T(8,128)(2,1)S(1)} %get-tuple-element.28), channel_id=1, source_target_pairs={{0,0},{1,8},{2,2},{3,10},{4,4},{5,12},{6,6},{7,14},{8,16},{9,24},{... | collective-permute-start | bytes 1572872 | tf_op jit(solution)/shard_map/ppermute | solution.py:132
  296.6 25.6 %collective-permute-start.14 = (bf16[128,2048]{0,1:T(8,128)(2,1)S(1)}, bf16[128,2048]{0,1:T(8,128)(2,1)S(1)}, u32[]{:S(2)}, u32[]{:S(2)}) collective-permute-start(bf16[128,2048]{0,1:T(8,128)(2,1)S(1)} %get-tuple-element.29), channel_id=1, source_target_pairs={{0,8},{1,0},{2,10},{3,2},{4,12},{5,4},{6,14},{7,6},{8,24},{9,16},{... | collective-permute-start | bytes 1572872 | tf_op jit(solution)/shard_map/ppermute | solution.py:132
  301.6 11.0 %collective-permute-start.17 = (f32[256,128]{1,0:T(8,128)S(1)}, f32[256,128]{1,0:T(8,128)S(1)}, u32[]{:S(2)}, u32[]{:S(2)}) collective-permute-start(f32[256,128]{1,0:T(8,128)S(1)} %pad_maximum_fusion.7), channel_id=1, source_target_pairs={{0,1},{1,0},{2,3},{3,2},{4,5},{5,4},{6,7},{7,6},{8,9},{9,8},{10,11... | collective-permute-start | bytes 393224 | tf_op jit(solution)/shard_map/ppermute | solution.py:140
Sparse Core Ops, SparseCore 0:
  138.7 23.6 all-gather.1

commit v3 on v0

--- a/solution.py
+++ b/solution.py
@@ -10,7 +10,7 @@
     )
 
 
-def body(proj_grads, val_grads):
+def general_body(proj_grads, val_grads):
     row_count = proj_grads.shape[0]
     pair_weight = 1.0 / row_count**0.5
     dp_index = lax.axis_index("dp")
@@ -32,9 +32,146 @@
     return (pair_values.astype(jnp.bfloat16), data_scores)
 
 
+ROWS_OF = ((0, 1), (2, 3), (1, 0), (3, 2))
+
+
+def split_body(proj_grads, val_grads):
+    row_count, width = proj_grads.shape
+    pair_weight = 1.0 / row_count**0.5
+    dp_index = lax.axis_index("dp")
+    feat_index = lax.axis_index("feat")
+    part, side, core = dp_index // 4, dp_index // 2 % 2, dp_index % 2
+    is_inner = (part == 1) | (part == 2)
+    both = ("dp", "feat")
+
+    def at(part, side, core):
+        return (part * 2 + side) * 2 + core
+
+    def moves(to, parts=range(4)):
+        return [
+            (at(p, s, c), at(*to(p, s, c))) for p in parts for s in (0, 1) for c in (0, 1)
+        ]
+
+    core_swap = moves(lambda p, s, c: (p, s, 1 - c))
+    side_swap = moves(lambda p, s, c: (p, 1 - s, c))
+    part_swap = moves(lambda p, s, c: (p ^ 1, s, c))
+    near_swap = moves(lambda p, s, c: (3 - p, s, c), (1, 2))
+    far_move = moves(lambda p, s, c: (2 if p == 0 else 1, s, c), (0, 3))
+    feat_swap = [(0, 1), (1, 0)]
+
+    def ordered(flag, mine, other, axis):
+        low = jnp.where(flag == 0, mine, other)
+        high = jnp.where(flag == 0, other, mine)
+        return jnp.concatenate([low, high], axis)
+
+    half_width, piece = width // 2, row_count // 2
+    mine = lax.dynamic_slice_in_dim(proj_grads, core * half_width, half_width, 1)
+    give = lax.dynamic_slice_in_dim(proj_grads, (1 - core) * half_width, half_width, 1)
+    other = lax.ppermute(give, "dp", core_swap)
+    own = [ordered(core, mine[:piece], other[:piece], 0), ordered(core, mine[piece:], other[piece:], 0)]
+
+    by_part = [lax.ppermute(rows, "dp", part_swap) for rows in own]
+    by_side = [lax.ppermute(rows, "dp", side_swap) for rows in own]
+    near = [lax.ppermute(rows, "dp", near_swap) for rows in own]
+    first_part = jnp.dot(proj_grads, val_grads, preferred_element_type=jnp.float32)
+    first_local = first_part + lax.ppermute(first_part, "feat", feat_swap)
+
+    far_0, by_both_0, far_1, by_both_1, first_local = lax.optimization_barrier(
+        (own[0], by_part[0], own[1], by_part[1], first_local)
+    )
+    far_0 = lax.ppermute(far_0, "dp", far_move)
+    by_both_0 = lax.ppermute(by_both_0, "dp", side_swap)
+    half = lax.axis_size("dp") // 2
+    first_half = lax.all_gather(
+        first_local, "dp", axis=0, tiled=True,
+        axis_index_groups=[list(range(half)), list(range(half, 2 * half))],
+    )
+
+    def summed(rows, cols):
+        tile = jnp.concatenate(
+            [jnp.concatenate([pair_tile(r, c) for c in cols], 1) for r in rows], 0
+        )
+        tile = tile.reshape(len(rows), 2, piece, tile.shape[1])
+        keep = lax.dynamic_index_in_dim(tile, core, 1, False)
+        send = lax.dynamic_index_in_dim(tile, 1 - core, 1, False)
+        tile = keep + lax.ppermute(send, "dp", core_swap)
+        tile = tile.reshape(len(rows), 2, piece // 2, tile.shape[2])
+        keep = lax.dynamic_index_in_dim(tile, feat_index, 1, False)
+        send = lax.dynamic_index_in_dim(tile, 1 - feat_index, 1, False)
+        tile = keep + lax.ppermute(send, "feat", feat_swap)
+        return tile.reshape(-1, tile.shape[2])
+
+    rows_a = [jnp.where(is_inner, n, o) for n, o in zip(near, own)]
+    cols = own + by_side + by_part
+    gram_a = summed(rows_a, cols)
+    far_0, by_both_0, far_1, by_both_1 = lax.optimization_barrier(
+        (far_0, by_both_0, far_1, by_both_1)
+    )
+    far_1 = lax.ppermute(far_1, "dp", far_move)
+    by_both_1 = lax.ppermute(by_both_1, "dp", side_swap)
+    rows_b0 = jnp.where(is_inner, far_0, by_part[0])
+    gram_b0 = summed([rows_b0], cols)
+    gram_c0 = summed(rows_a + [rows_b0], [by_both_0])
+    far_1, by_both_1, gram_a, gram_b0, gram_c0, first_half = lax.optimization_barrier(
+        (far_1, by_both_1, gram_a, gram_b0, gram_c0, first_half)
+    )
+    gram_c1 = summed(rows_a + [rows_b0], [by_both_1])
+    rows_b1 = jnp.where(is_inner, far_1, by_part[1])
+    gram_b1 = summed([rows_b1], cols + [by_both_0, by_both_1])
+
+    rows_of = jnp.asarray(ROWS_OF, jnp.int32)[part]
+    offsets = jnp.concatenate(
+        [c * piece + feat_index * (piece // 2) + jnp.arange(piece // 2, dtype=jnp.int32) for c in (0, 1)]
+    )
+
+    def finished(tile, which):
+        col_count = tile.shape[1]
+        block = piece
+        chips = []
+        for chip in range(4):
+            part_of = [
+                tile[:, (chip * 4 + k) * block:(chip * 4 + k + 1) * block] for k in (0, 2, 1, 3)
+            ]
+            chips.append(jnp.concatenate(part_of, 1))
+        tile = ordered(
+            part % 2, ordered(side, chips[0], chips[1], 1), ordered(side, chips[2], chips[3], 1), 1
+        )
+        row_ids = ((rows_of[which] * 2 + side) * 2 + core) * row_count + offsets
+        col_ids = (part // 2) * col_count + jnp.arange(col_count, dtype=jnp.int32)
+        values = jnp.where(row_ids[:, None] == col_ids[None, :], 0.0, tile)
+        return values, jnp.dot(values, first_half, precision=lax.Precision.HIGHEST)
+
+    def deliver(values, which):
+        return [
+            lax.ppermute(values, both, [
+                (at(p, s, c) * 2 + f, at(ROWS_OF[p][which], s, c) * 2 + p // 2)
+                for p in range(4) for s in (0, 1) for c in (0, 1)
+            ])
+            for f in (0, 1)
+        ]
+
+    def placed(from_a, from_b):
+        takes_a = (part + feat_index) % 2 == 0
+        low, high = (jnp.where(takes_a, a, b) for a, b in zip(from_a, from_b))
+        rows = piece // 2
+        return jnp.concatenate([low[:rows], high[:rows], low[rows:], high[rows:]], 0)
+
+    kept = gram_c0.shape[0] * 2 // 3
+    values_a, sums_a = finished(jnp.concatenate([gram_a, gram_c0[:kept], gram_c1[:kept]], 1), 0)
+    sent_a = deliver(values_a.astype(jnp.bfloat16), 0)
+    sent_sums_a = deliver(sums_a, 0)
+    rows_0 = jnp.concatenate([gram_b0, gram_c0[kept:], gram_c1[kept:]], 1)
+    values_b, sums_b = finished(jnp.concatenate([rows_0, gram_b1], 0), 1)
+    half_sum = placed(sent_sums_a, deliver(sums_b, 1))
+    interactions = placed(sent_a, deliver(values_b.astype(jnp.bfloat16), 1))
+    pair_sum = half_sum + lax.ppermute(half_sum, "feat", feat_swap)
+    return (interactions, first_local - pair_weight * pair_sum)
+
+
 def solution(mesh):
+    split = mesh.shape["feat"] == 2 and mesh.shape["dp"] == 16
     return jax.shard_map(
-        body,
+        split_body if split else general_body,
         mesh=mesh,
         in_specs=(P("dp", "feat"), P("feat", None)),
         out_specs=(P("dp", "feat"), P("dp", None)),

time: 463 us -> 368 us (0.79); the launches traced: 461 us -> 362 us
  waiting for transfers between devices: 402 us -> 168 us
  starting transfers between devices: 0.2 us -> 45.4 us
  local copies, waits for them, and re-layouts: 1.55 us -> 39.1 us
  matrix products: 37.8 us -> 65.1 us
  other arithmetic: 4.42 us -> 27.9 us
    all_gather x2 -> x1, waiting for transfers between devices: 318 us -> 0.02 us  [split_body(): lax.all_gather(first_local, 'dp', axis=0, tiled=True, axis_index_groups=[...]
    ppermute x0 -> x31, waiting for transfers between devices: none -> 168 us  [the longest x2 44.2 us: split_body(): by_part = [lax.ppermute(rows, 'dp', part_swap) for rows in own]]
    ppermute x0 -> x31, starting transfers between devices: none -> 45.3 us  [the longest x8 19.6 us: deliver(): lax.ppermute(values, both, [(at(p, s, c) * 2 + f, at(ROWS_OF[p][which], s...]
    reduce_scatter x1 -> x0, waiting for transfers between devices: 42.7 us -> none  [body(): lax.psum_scatter(block_row, 'feat', scatter_dimension=1, tiled=True)]
    psum x2 -> x0, waiting for transfers between devices: 40.8 us -> none  [the longest x1 22 us: body(): lax.psum(jnp.dot(proj_grads, val_grads, preferred_element_type=jnp.float3...]
    dot_general x1 -> x32, matrix products: 29.3 us -> 61.3 us  [pair_tile(): lax.dot_general(left_rows, right_rows, (((1,), (1,)), ((), ())), preferre...]
    dynamic_slice x0 -> x5, local copies, waits for them, and re-layouts: none -> 21.1 us  [the longest x2 12.2 us: summed(): keep = lax.dynamic_index_in_dim(tile, core, 1, False)]
    select_n x0 -> x15, other arithmetic: none -> 13.8 us  [the longest x2 5.35 us: split_body(): rows_a = [jnp.where(is_inner, n, o) for n, o in zip(near, own)]]
  transfers between devices with their start and end apart: 5 -> 32, of which waited for: 5 -> 16; matrix products, arithmetic and copies ran while one was open for 7% -> 30% of each run, Pallas kernels for 0% -> 0%
where the time goes in v3:
time: 368 us; the launch traced here: 362 us
  waiting for transfers between devices  168 us (46%)
  matrix products  65.1 us (18%)
  starting transfers between devices  45.4 us (12%)
  local copies, waits for them, and re-layouts  39.1 us (11%)
  other arithmetic  27.9 us (8%)
  between operations  16.6 us (5%)
    dot_general x32, matrix products, pair_tile(): lax.dot_general(left_rows, right_rows, (((1,), (1,)), ((), ())), preferre...  61.3 us
    ppermute x2, waiting for transfers between devices, split_body(): by_part = [lax.ppermute(rows, 'dp', part_swap) for rows in own]  44.2 us
    ppermute x5, waiting for transfers between devices, summed(): tile = keep + lax.ppermute(send, 'feat', feat_swap)  36.3 us
    ppermute x2, waiting for transfers between devices, split_body(): near = [lax.ppermute(rows, 'dp', near_swap) for rows in own]  34.7 us
    ppermute x8, starting transfers between devices, deliver(): lax.ppermute(values, both, [(at(p, s, c) * 2 + f, at(ROWS_OF[p][which], s...  19.6 us
    ppermute x1, waiting for transfers between devices, split_body(): far_1 = lax.ppermute(far_1, 'dp', far_move)  19.3 us
    dynamic_slice x2, local copies, waits for them, and re-layouts, summed(): keep = lax.dynamic_index_in_dim(tile, core, 1, False)  12.2 us
    reshape x3, local copies, waits for them, and re-layouts, summed(): tile = tile.reshape(len(rows), 2, piece, tile.shape[1])  10.4 us
  transfers between devices with their start and end apart: 32, of which 16 were waited for; matrix products, arithmetic and copies ran while one was open for 30% of the time, Pallas kernels for 0%

profile of v3, /device:TPU:18, one launch (start us, length us, event | category | flops | bytes accessed | tf_op | source)
XLA Modules:
  0.0 361.6 jit_solution(2669079575988755402)
XLA Ops:
  7.2 3.3 constant_dynamic-slice_fusion.2
  10.5 4.5 %collective-permute-done = bf16[256,4096]{1,0:T(8,128)(2,1)} collective-permute-done((bf16[256,4096]{1,0:T(8,128)(2,1)}, bf16[256,4096]{1,0:T(8,128)(2,1)}, u32[]{:S(2)}, u32[]{:S(2)}) %collective-permute-start) | collective-permute-done | bytes 2097184 | tf_op jit(solution)/shard_map/ppermute | solution.py:70
  15.0 4.2 %broadcast_select_fusion.5 = (bf16[128,4096]{1,0:T(8,128)(2,1)S(1)}, bf16[128,4096]{1,0:T(8,128)(2,1)S(1)}, bf16[128,4096]{1,0:T(8,128)(2,1)}, bf16[128,4096]{1,0:T(8,128)(2,1)S(1)}) fusion(pred[]{:T(512)S(6)} %eq.35, bf16[256,4096]{1,0:T(8,128)(2,1)} %collective-permute-done, bf16[256,8192]{1,0:T(8,128)(2,1)} %param.3, s32[]{:T(128)S(6)} %add.206, ...), kind=kLoop, calls=%fused_computation.41 | loop fusion | flops 2097152 | bytes 8388617 | tf_op jit(solution)/shard_map/jit(_where)/select_n | solution.py:63
  19.2 1.5 pad_maximum_fusion.1
  21.3 2.5 collective-permute-start.8
  25.2 1.6 collective-permute-start.3
  30.6 2.7 pad_maximum_fusion.2
  33.3 2.3 collective-permute-start.11
  37.4 34.6 %collective-permute-done.8 = bf16[256,4096]{1,0:T(8,128)(2,1)} collective-permute-done((bf16[256,4096]{1,0:T(8,128)(2,1)}, bf16[256,4096]{1,0:T(8,128)(2,1)}, u32[]{:S(2)}, u32[]{:S(2)}) %collective-permute-start.8) | collective-permute-done | bytes 2097184 | tf_op jit(solution)/shard_map/ppermute | solution.py:75
  72.6 3.0 broadcast_select_fusion.3
  78.3 43.5 %collective-permute-done.2 = bf16[256,4096]{1,0:T(8,128)(2,1)} collective-permute-done((bf16[256,4096]{1,0:T(8,128)(2,1)}, bf16[256,4096]{1,0:T(8,128)(2,1)}, u32[]{:S(2)}, u32[]{:S(2)}) %collective-permute-start.2) | collective-permute-done | bytes 2097184 | tf_op jit(solution)/shard_map/ppermute | solution.py:73
  121.8 1.8 collective-permute-start.4
  124.2 2.4 broadcast_select_fusion.2
  128.8 1.8 collective-permute-done.10
  131.4 2.3 convolution_dynamic-update-slice_fusion.21
  135.2 2.3 convolution_dynamic-update-slice_fusion.15
  137.6 2.3 convolution_dynamic-update-slice_fusion.14
  139.9 2.3 convolution_dynamic-update-slice_fusion.20
  142.3 2.1 pad_maximum_fusion
  144.4 5.4 %reshape.85 = f32[2,2,128,1536]{2,1,0,3:T(2,128)} reshape(f32[512,1536]{0,1:T(8,128)} %pad_maximum_fusion) | data formatting | bytes 6291456 | tf_op jit(solution)/shard_map/reshape | solution.py:94
  149.8 7.3 %constant_dynamic-slice_fusion.1 = (f32[2,1,128,1536]{2,1,0,3:T(1,128)}, f32[2,1,128,1536]{2,1,0,3:T(1,128)}) fusion(f32[2,2,128,1536]{2,1,0,3:T(2,128)} %reshape.85, s32[]{:T(128)S(6)} %select_n.227, s32[]{:T(128)S(6)} %select_n.228), kind=kLoop, calls=%fused_computation.107 | loop fusion | bytes 6291464 | tf_op jit(solution)/shard_map/jit(dynamic_index_in_dim)/dynamic_slice | solution.py:95
  157.1 4.9 %copy.5 = f32[2,1,128,1536]{3,2,0,1:T(8,128)} copy(f32[2,1,128,1536]{2,1,0,3:T(1,128)} %get-tuple-element.36) | data formatting | bytes 3145728 | tf_op jit(solution)/shard_map/jit(dynamic_index_in_dim)/dynamic_slice | solution.py:95
  162.0 4.9 %copy.6 = f32[2,1,128,1536]{3,2,0,1:T(8,128)} copy(f32[2,1,128,1536]{2,1,0,3:T(1,128)} %get-tuple-element.37) | data formatting | bytes 3145728 | tf_op jit(solution)/shard_map/jit(dynamic_index_in_dim)/dynamic_slice | solution.py:96
  166.9 4.1 %collective-permute-done.4 = bf16[256,4096]{1,0:T(8,128)(2,1)} collective-permute-done((bf16[256,4096]{1,0:T(8,128)(2,1)}, bf16[256,4096]{1,0:T(8,128)(2,1)}, u32[]{:S(2)}, u32[]{:S(2)}) %collective-permute-start.4) | collective-permute-done | bytes 2097184 | tf_op jit(solution)/shard_map/ppermute | solution.py:82
  171.1 4.3 %collective-permute-done.5 = bf16[256,4096]{1,0:T(8,128)(2,1)} collective-permute-done((bf16[256,4096]{1,0:T(8,128)(2,1)}, bf16[256,4096]{1,0:T(8,128)(2,1)}, u32[]{:S(2)}, u32[]{:S(2)}) %collective-permute-start.5) | collective-permute-done | bytes 2097184 | tf_op jit(solution)/shard_map/ppermute | solution.py:83
  175.4 3.0 fusion.39
  178.4 2.3 fusion.38
  180.7 1.8 broadcast_select_fusion.1
  182.6 3.1 fusion.40
  185.7 1.4 convolution_dynamic-update-slice_fusion.13
  188.8 1.5 convolution_dynamic-update-slice_fusion.12
  193.3 3.0 convolution_dynamic-update-slice_fusion.9
  196.3 3.0 convolution_dynamic-update-slice_fusion.8
  199.4 3.1 copy.11
  204.1 1.7 bitcast_add_fusion
  206.1 1.6 collective-permute-start.6
  208.0 1.9 collective-permute-start.17
  210.3 16.0 %collective-permute-done.13 = f32[2,64,1536]{2,1,0:T(8,128)S(1)} collective-permute-done((f32[2,64,1536]{2,1,0:T(8,128)S(1)}, f32[2,64,1536]{2,1,0:T(8,128)S(1)}, u32[]{:S(2)}, u32[]{:S(2)}) %collective-permute-start.13) | collective-permute-done | bytes 786464 | tf_op jit(solution)/shard_map/ppermute | solution.py:101
  227.3 3.2 collective-permute-done.17
  231.2 7.1 %collective-permute-done.15 = f32[1,64,1536]{2,1,0:T(8,128)S(1)} collective-permute-done((f32[1,64,1536]{2,1,0:T(8,128)S(1)}, f32[1,64,1536]{2,1,0:T(8,128)S(1)}, u32[]{:S(2)}, u32[]{:S(2)}) %collective-permute-start.15) | collective-permute-done | bytes 393248 | tf_op jit(solution)/shard_map/ppermute | solution.py:101
  238.3 19.3 %collective-permute-done.6 = bf16[256,4096]{1,0:T(8,128)(2,1)} collective-permute-done((bf16[256,4096]{1,0:T(8,128)(2,1)}, bf16[256,4096]{1,0:T(8,128)(2,1)}, u32[]{:S(2)}, u32[]{:S(2)}) %collective-permute-start.6) | collective-permute-done | bytes 2097184 | tf_op jit(solution)/shard_map/ppermute | solution.py:110
  257.6 3.1 fusion.43
  260.8 2.3 fusion.42
  263.1 2.3 fusion.41
  266.5 1.9 broadcast_select_fusion
  268.6 1.5 convolution_dynamic-update-slice_fusion.7
  270.0 1.5 convolution_dynamic-update-slice_fusion.6
  271.6 1.5 convolution_dynamic-update-slice_fusion.5
  274.7 3.0 convolution_dynamic-update-slice_fusion.3
  277.7 3.0 convolution_dynamic-update-slice_fusion.2
  280.7 3.0 convolution_dynamic-update-slice_fusion.1
  283.8 3.0 convolution_dynamic-update-slice_fusion
  286.8 1.9 copy.12
  290.9 1.6 collective-permute-start.19
  292.7 5.3 %collective-permute-done.19 = f32[3,64,256]{2,1,0:T(8,128)S(1)} collective-permute-done((f32[3,64,256]{2,1,0:T(8,128)S(1)}, f32[3,64,256]{2,1,0:T(8,128)S(1)}, u32[]{:S(2)}, u32[]{:S(2)}) %collective-permute-start.19) | collective-permute-done | bytes 196640 | tf_op jit(solution)/shard_map/ppermute | solution.py:101
  298.3 1.6 collective-permute-start.22
  302.5 5.7 %collective-permute-start.26 = (f32[128,128]{1,0:T(8,128)S(1)}, f32[128,128]{1,0:T(8,128)S(1)}, u32[]{:S(2)}, u32[]{:S(2)}) collective-permute-start(f32[128,128]{1,0:T(8,128)S(1)} %fusion.2), channel_id=1, source_target_pairs={{0,0},{2,2},{4,4},{6,6},{8,16},{10,18},{12,20},{14,22},{16,9},{18,... | collective-permute-start | bytes 196616 | tf_op jit(solution)/shard_map/ppermute | solution.py:146
  308.3 4.7 %collective-permute-done.22 = f32[1,64,2048]{2,1,0:T(8,128)S(1)} collective-permute-done((f32[1,64,2048]{2,1,0:T(8,128)S(1)}, f32[1,64,2048]{2,1,0:T(8,128)S(1)}, u32[]{:S(2)}, u32[]{:S(2)}) %collective-permute-start.22) | collective-permute-done | bytes 524320 | tf_op jit(solution)/shard_map/ppermute | solution.py:101
  315.7 6.6 %collective-permute-start.27 = (f32[128,128]{1,0:T(8,128)S(1)}, f32[128,128]{1,0:T(8,128)S(1)}, u32[]{:S(2)}, u32[]{:S(2)}) collective-permute-start(f32[128,128]{1,0:T(8,128)S(1)} %fusion), channel_id=1, source_target_pairs={{0,8},{2,10},{4,12},{6,14},{8,24},{10,26},{12,28},{14,30},{16,1},{... | collective-permute-start | bytes 196616 | tf_op jit(solution)/shard_map/ppermute | solution.py:146
  324.5 6.4 %collective-permute-start.30 = (f32[256,128]{1,0:T(8,128)S(1)}, f32[256,128]{1,0:T(8,128)S(1)}, u32[]{:S(2)}, u32[]{:S(2)}) collective-permute-start(f32[256,128]{1,0:T(8,128)S(1)} %pad_maximum_fusion.19), channel_id=1, source_target_pairs={{0,1},{1,0},{2,3},{3,2},{4,5},{5,4},{6,7},{7,6},{8,9},{9,8},{10,11... | collective-permute-start | bytes 393224 | tf_op jit(solution)/shard_map/ppermute | solution.py:167
  332.2 1.9 collective-permute-start.20
  334.1 9.6 %collective-permute-done.30 = f32[256,128]{1,0:T(8,128)S(1)} collective-permute-done((f32[256,128]{1,0:T(8,128)S(1)}, f32[256,128]{1,0:T(8,128)S(1)}, u32[]{:S(2)}, u32[]{:S(2)}) %collective-permute-start.30) | collective-permute-done | bytes 131104 | tf_op jit(solution)/shard_map/ppermute | solution.py:167
  344.4 4.6 %collective-permute-done.24 = bf16[128,2048]{1,0:T(8,128)(2,1)S(1)} collective-permute-done((bf16[128,2048]{1,0:T(8,128)(2,1)S(1)}, bf16[128,2048]{1,0:T(8,128)(2,1)S(1)}, u32[]{:S(2)}, u32[]{:S(2)}) %collective-permute-start.24) | collective-permute-done | bytes 524320 | tf_op jit(solution)/shard_map/ppermute | solution.py:146
  349.2 4.2 %collective-permute-done.20 = bf16[128,2048]{1,0:T(8,128)(2,1)S(1)} collective-permute-done((bf16[128,2048]{1,0:T(8,128)(2,1)S(1)}, bf16[128,2048]{1,0:T(8,128)(2,1)S(1)}, u32[]{:S(2)}, u32[]{:S(2)}) %collective-permute-start.20) | collective-permute-done | bytes 524320 | tf_op jit(solution)/shard_map/ppermute | solution.py:146
  (170 shorter events, 39.5 us)
Async XLA Ops:
  7.2 16.6 %copy-start = (bf16[8192,128]{1,0:T(8,128)(2,1)S(1)}, bf16[8192,128]{1,0:T(8,128)(2,1)}, u32[]{:S(2)}) copy-start(bf16[8192,128]{1,0:T(8,128)(2,1)} %param.4) | copy-start | bytes 6291460
  7.2 231.1 %all-gather.2.cloned.1.call-start = ((), (), s32[]{:S(2)}) async-start(), calls=%async_computation | async-start | bytes 1179648 | tf_op jit(solution)/shard_map/all_gather | solution.py:85
  10.5 4.5 %collective-permute-start = (bf16[256,4096]{1,0:T(8,128)(2,1)}, bf16[256,4096]{1,0:T(8,128)(2,1)}, u32[]{:S(2)}, u32[]{:S(2)}) collective-permute-start(bf16[256,4096]{1,0:T(8,128)(2,1)} %constant_dynamic-slice_fusion.2), channel_id=1, source_target_pairs={{0,2},{2,0},{4,6},{6,4},{8,10},{10,8},{12,14},{14,12},{16,18},{18,... | collective-permute-start | bytes 6291464 | tf_op jit(solution)/shard_map/ppermute | solution.py:70
  19.2 1.8 copy-start.9
  19.2 2.1 copy-start.13
  19.2 4.6 %copy-start.5 = (bf16[256,8192]{1,0:T(8,128)(2,1)S(1)}, bf16[256,8192]{1,0:T(8,128)(2,1)}, u32[]{:S(2)}) copy-start(bf16[256,8192]{1,0:T(8,128)(2,1)} %param.3) | copy-start | bytes 12582916
  21.3 50.8 %collective-permute-start.8 = (bf16[256,4096]{1,0:T(8,128)(2,1)}, bf16[256,4096]{1,0:T(8,128)(2,1)}, u32[]{:S(2)}, u32[]{:S(2)}) collective-permute-start(bf16[256,4096]{1,0:T(8,128)(2,1)} %pad_maximum_fusion.1), channel_id=1, source_target_pairs={{8,16},{10,18},{12,20},{14,22},{16,8},{18,10},{20,12},{22,14},{9,1... | collective-permute-start | bytes 6291464 | tf_op jit(solution)/shard_map/ppermute | solution.py:75
  25.2 11.1 %collective-permute-start.3 = (f32[256,128]{1,0:T(8,128)S(1)}, f32[256,128]{1,0:T(8,128)S(1)}, u32[]{:S(2)}, u32[]{:S(2)}) collective-permute-start(f32[256,128]{1,0:T(8,128)S(1)} %fusion.37), channel_id=1, source_target_pairs={{0,1},{1,0},{2,3},{3,2},{4,5},{5,4},{6,7},{7,6},{8,9},{9,8},{10,11... | collective-permute-start | bytes 393224 | tf_op jit(solution)/shard_map/ppermute | solution.py:77
  29.3 48.9 %collective-permute-start.1 = (bf16[256,4096]{1,0:T(8,128)(2,1)}, bf16[256,4096]{1,0:T(8,128)(2,1)}, u32[]{:S(2)}, u32[]{:S(2)}) collective-permute-start(bf16[256,4096]{1,0:T(8,128)(2,1)} %pad_maximum_fusion.1), channel_id=1, source_target_pairs={{0,8},{2,10},{4,12},{6,14},{8,0},{10,2},{12,4},{14,6},{16,24},{18,... | collective-permute-start | bytes 6291464 | tf_op jit(solution)/shard_map/ppermute | solution.py:73
  33.3 90.9 %collective-permute-start.11 = (bf16[256,4096]{1,0:T(8,128)(2,1)}, bf16[256,4096]{1,0:T(8,128)(2,1)}, u32[]{:S(2)}, u32[]{:S(2)}) collective-permute-start(bf16[256,4096]{1,0:T(8,128)(2,1)} %pad_maximum_fusion.2), channel_id=1, source_target_pairs={{8,16},{10,18},{12,20},{14,22},{16,8},{18,10},{20,12},{22,14},{9,1... | collective-permute-start | bytes 6291464 | tf_op jit(solution)/shard_map/ppermute | solution.py:75
  35.6 86.2 %collective-permute-start.2 = (bf16[256,4096]{1,0:T(8,128)(2,1)}, bf16[256,4096]{1,0:T(8,128)(2,1)}, u32[]{:S(2)}, u32[]{:S(2)}) collective-permute-start(bf16[256,4096]{1,0:T(8,128)(2,1)} %pad_maximum_fusion.2), channel_id=1, source_target_pairs={{0,8},{2,10},{4,12},{6,14},{8,0},{10,2},{12,4},{14,6},{16,24},{18,... | collective-permute-start | bytes 6291464 | tf_op jit(solution)/shard_map/ppermute | solution.py:73
  36.9 38.7 %copy-start.10 = (bf16[128,4096]{1,0:T(8,128)(2,1)S(1)}, bf16[128,4096]{1,0:T(8,128)(2,1)}, u32[]{:S(2)}) copy-start(bf16[128,4096]{1,0:T(8,128)(2,1)} %copy-done.9) | copy-start | bytes 3145732
  36.9 38.7 %copy-start.14 = (bf16[128,4096]{1,0:T(8,128)(2,1)S(1)}, bf16[128,4096]{1,0:T(8,128)(2,1)}, u32[]{:S(2)}) copy-start(bf16[128,4096]{1,0:T(8,128)(2,1)} %copy-done.13) | copy-start | bytes 3145732
  36.9 91.2 %collective-permute-start.9 = (bf16[256,4096]{1,0:T(8,128)(2,1)}, bf16[256,4096]{1,0:T(8,128)(2,1)S(1)}, u32[]{:S(2)}, u32[]{:S(2)}) collective-permute-start(bf16[256,4096]{1,0:T(8,128)(2,1)} %pad_maximum_fusion.1), channel_id=1, source_target_pairs={{0,4},{2,6},{4,0},{6,2},{8,12},{10,14},{12,8},{14,10},{16,20},{18,... | collective-permute-start | bytes 6291464 | tf_op jit(solution)/shard_map/ppermute | solution.py:74
  72.1 58.5 %collective-permute-start.10 = (bf16[256,4096]{1,0:T(8,128)(2,1)}, bf16[256,4096]{1,0:T(8,128)(2,1)S(1)}, u32[]{:S(2)}, u32[]{:S(2)}) collective-permute-start(bf16[256,4096]{1,0:T(8,128)(2,1)} %pad_maximum_fusion.2), channel_id=1, source_target_pairs={{0,4},{2,6},{4,0},{6,2},{8,12},{10,14},{12,8},{14,10},{16,20},{18,... | collective-permute-start | bytes 6291464 | tf_op jit(solution)/shard_map/ppermute | solution.py:74
  75.6 1.2 copy-start.6
  121.8 49.3 %collective-permute-start.4 = (bf16[256,4096]{1,0:T(8,128)(2,1)}, bf16[256,4096]{1,0:T(8,128)(2,1)}, u32[]{:S(2)}, u32[]{:S(2)}) collective-permute-start(bf16[256,4096]{1,0:T(8,128)(2,1)} %pad_maximum_fusion.1), channel_id=1, source_target_pairs={{0,16},{2,18},{4,20},{6,22},{24,8},{26,10},{28,12},{30,14},{1,17},... | collective-permute-start | bytes 6291464 | tf_op jit(solution)/shard_map/ppermute | solution.py:82
  123.6 51.8 %collective-permute-start.5 = (bf16[256,4096]{1,0:T(8,128)(2,1)}, bf16[256,4096]{1,0:T(8,128)(2,1)}, u32[]{:S(2)}, u32[]{:S(2)}) collective-permute-start(bf16[256,4096]{1,0:T(8,128)(2,1)} %collective-permute-done.1), channel_id=1, source_target_pairs={{0,4},{2,6},{4,0},{6,2},{8,12},{10,14},{12,8},{14,10},{16,20},{18,... | collective-permute-start | bytes 6291464 | tf_op jit(solution)/shard_map/ppermute | solution.py:83
  126.6 11.0 %copy-start.2 = (bf16[256,4096]{1,0:T(8,128)(2,1)}, bf16[256,4096]{1,0:T(8,128)(2,1)S(1)}, u32[]{:S(2)}) copy-start(bf16[256,4096]{1,0:T(8,128)(2,1)S(1)} %broadcast_select_fusion.2) | copy-start | bytes 6291460
  128.1 5.6 %copy-start.27 = (bf16[256,4096]{1,0:T(8,128)(2,1)}, bf16[256,4096]{1,0:T(8,128)(2,1)S(1)}, u32[]{:S(2)}) copy-start(bf16[256,4096]{1,0:T(8,128)(2,1)S(1)} %collective-permute-done.9) | copy-start | bytes 6291460
  130.6 3.8 %copy-start.30 = (bf16[256,4096]{1,0:T(8,128)(2,1)}, bf16[256,4096]{1,0:T(8,128)(2,1)S(1)}, u32[]{:S(2)}) copy-start(bf16[256,4096]{1,0:T(8,128)(2,1)S(1)} %collective-permute-done.10) | copy-start | bytes 6291460
  166.9 36.9 %collective-permute-start.12 = (f32[2,128,1536]{2,1,0:T(8,128)}, f32[2,128,1536]{2,1,0:T(8,128)}, u32[]{:S(2)}, u32[]{:S(2)}) collective-permute-start(f32[2,128,1536]{2,1,0:T(8,128)} %bitcast.140), channel_id=1, source_target_pairs={{0,2},{2,0},{4,6},{6,4},{8,10},{10,8},{12,14},{14,12},{16,18},{18,... | collective-permute-start | bytes 4718600 | tf_op jit(solution)/shard_map/ppermute | solution.py:97
  182.6 13.8 %copy-start.4 = (bf16[256,4096]{1,0:T(8,128)(2,1)}, bf16[256,4096]{1,0:T(8,128)(2,1)S(1)}, u32[]{:S(2)}) copy-start(bf16[256,4096]{1,0:T(8,128)(2,1)S(1)} %broadcast_select_fusion.1) | copy-start | bytes 6291460
  182.6 3.1 copy-start.11
  182.6 3.1 copy-start.15
  187.2 1.6 copy-start.7
  187.2 3.0 copy-start.21
  188.0 2.3 copy-start.28
  188.0 19.9 %collective-permute-start.16 = (f32[3,128,256]{2,1,0:T(8,128)}, f32[3,128,256]{2,1,0:T(8,128)S(1)}, u32[]{:S(2)}, u32[]{:S(2)}) collective-permute-start(f32[3,128,256]{2,1,0:T(8,128)} %dynamic-slice_bitcast_fusion.5), channel_id=1, source_target_pairs={{0,2},{2,0},{4,6},{6,4},{8,10},{10,8},{12,14},{14,12},{16,18},{18,... | collective-permute-start | bytes 1179656 | tf_op jit(solution)/shard_map/ppermute | solution.py:97
  190.3 1.6 copy-start.31
  202.4 1.6 copy-start.18
  203.8 4.1 %copy-start.22 = (f32[768,256]{1,0:T(8,128)S(1)}, f32[768,256]{1,0:T(8,128)}, u32[]{:S(2)}) copy-start(f32[768,256]{1,0:T(8,128)} %copy-done.21) | copy-start | bytes 2359300
  203.8 6.1 %collective-permute-start.14 = (f32[1,128,1536]{2,1,0:T(8,128)S(1)}, f32[1,128,1536]{2,1,0:T(8,128)S(1)}, u32[]{:S(2)}, u32[]{:S(2)}) collective-permute-start(f32[1,128,1536]{2,1,0:T(8,128)S(1)} %dynamic-slice_bitcast_fusion.1), channel_id=1, source_target_pairs={{0,2},{2,0},{4,6},{6,4},{8,10},{10,8},{12,14},{14,12},{16,18},{18,... | collective-permute-start | bytes 2359304 | tf_op jit(solution)/shard_map/ppermute | solution.py:97
  205.8 4.2 %copy-start.17 = (f32[256,1536]{1,0:T(8,128)S(1)}, f32[256,1536]{1,0:T(8,128)}, u32[]{:S(2)}) copy-start(f32[256,1536]{1,0:T(8,128)} %copy.11) | copy-start | bytes 4718596
  205.8 20.4 %collective-permute-start.13 = (f32[2,64,1536]{2,1,0:T(8,128)S(1)}, f32[2,64,1536]{2,1,0:T(8,128)S(1)}, u32[]{:S(2)}, u32[]{:S(2)}) collective-permute-start(f32[2,64,1536]{2,1,0:T(8,128)S(1)} %dynamic-slice_bitcast_fusion.2), channel_id=1, source_target_pairs={{0,1},{1,0},{2,3},{3,2},{4,5},{5,4},{6,7},{7,6},{8,9},{9,8},{10,11... | collective-permute-start | bytes 2359304 | tf_op jit(solution)/shard_map/ppermute | solution.py:101
  206.1 51.5 %collective-permute-start.6 = (bf16[256,4096]{1,0:T(8,128)(2,1)}, bf16[256,4096]{1,0:T(8,128)(2,1)}, u32[]{:S(2)}, u32[]{:S(2)}) collective-permute-start(bf16[256,4096]{1,0:T(8,128)(2,1)} %pad_maximum_fusion.2), channel_id=1, source_target_pairs={{0,16},{2,18},{4,20},{6,22},{24,8},{26,10},{28,12},{30,14},{1,17},... | collective-permute-start | bytes 6291464 | tf_op jit(solution)/shard_map/ppermute | solution.py:110
  207.8 49.9 %collective-permute-start.7 = (bf16[256,4096]{1,0:T(8,128)(2,1)}, bf16[256,4096]{1,0:T(8,128)(2,1)}, u32[]{:S(2)}, u32[]{:S(2)}) collective-permute-start(bf16[256,4096]{1,0:T(8,128)(2,1)} %collective-permute-done.2), channel_id=1, source_target_pairs={{0,4},{2,6},{4,0},{6,2},{8,12},{10,14},{12,8},{14,10},{16,20},{18,... | collective-permute-start | bytes 6291464 | tf_op jit(solution)/shard_map/ppermute | solution.py:111
  208.0 22.5 %collective-permute-start.17 = (f32[3,64,256]{2,1,0:T(8,128)S(1)}, f32[3,64,256]{2,1,0:T(8,128)S(1)}, u32[]{:S(2)}, u32[]{:S(2)}) collective-permute-start(f32[3,64,256]{2,1,0:T(8,128)S(1)} %dynamic-slice_bitcast_fusion.8), channel_id=1, source_target_pairs={{0,1},{1,0},{2,3},{3,2},{4,5},{5,4},{6,7},{7,6},{8,9},{9,8},{10,11... | collective-permute-start | bytes 589832 | tf_op jit(solution)/shard_map/ppermute | solution.py:101
  210.1 28.2 %collective-permute-start.15 = (f32[1,64,1536]{2,1,0:T(8,128)S(1)}, f32[1,64,1536]{2,1,0:T(8,128)S(1)}, u32[]{:S(2)}, u32[]{:S(2)}) collective-permute-start(f32[1,64,1536]{2,1,0:T(8,128)S(1)} %dynamic-slice_bitcast_fusion.6), channel_id=1, source_target_pairs={{0,1},{1,0},{2,3},{3,2},{4,5},{5,4},{6,7},{7,6},{8,9},{9,8},{10,11... | collective-permute-start | bytes 1179656 | tf_op jit(solution)/shard_map/ppermute | solution.py:101
  257.6 3.1 copy-start.3
  266.4 2.1 copy-start.12
  266.4 2.2 copy-start.16
  266.4 22.7 %collective-permute-start.18 = (f32[3,128,256]{2,1,0:T(8,128)}, f32[3,128,256]{2,1,0:T(8,128)}, u32[]{:S(2)}, u32[]{:S(2)}) collective-permute-start(f32[3,128,256]{2,1,0:T(8,128)} %dynamic-slice_bitcast_fusion.4), channel_id=1, source_target_pairs={{0,2},{2,0},{4,6},{6,4},{8,10},{10,8},{12,14},{14,12},{16,18},{18,... | collective-permute-start | bytes 1179656 | tf_op jit(solution)/shard_map/ppermute | solution.py:97
  268.6 1.5 copy-start.8
  270.0 1.6 copy-start.29
  271.6 1.6 copy-start.32
  288.7 1.1 copy-start.24
  288.7 3.8 %copy-start.20 = (f32[2,64,1536]{2,1,0:T(8,128)S(1)}, f32[2,64,1536]{2,1,0:T(8,128)}, u32[]{:S(2)}) copy-start(f32[2,64,1536]{2,1,0:T(8,128)} %bitcast_add_fusion.3) | copy-start | bytes 2359300
  288.7 3.8 %copy-start.26 = (f32[3,64,256]{2,1,0:T(8,128)S(1)}, f32[3,64,256]{2,1,0:T(8,128)}, u32[]{:S(2)}) copy-start(f32[3,64,256]{2,1,0:T(8,128)} %bitcast_add_fusion.9) | copy-start | bytes 589828
  288.8 9.3 %collective-permute-start.21 = (f32[1,128,2048]{2,1,0:T(8,128)S(1)}, f32[1,128,2048]{2,1,0:T(8,128)S(1)}, u32[]{:S(2)}, u32[]{:S(2)}) collective-permute-start(f32[1,128,2048]{2,1,0:T(8,128)S(1)} %dynamic-slice_bitcast_fusion), channel_id=1, source_target_pairs={{0,2},{2,0},{4,6},{6,4},{8,10},{10,8},{12,14},{14,12},{16,18},{18,... | collective-permute-start | bytes 3145736 | tf_op jit(solution)/shard_map/ppermute | solution.py:97
  290.9 7.1 %collective-permute-start.19 = (f32[3,64,256]{2,1,0:T(8,128)S(1)}, f32[3,64,256]{2,1,0:T(8,128)S(1)}, u32[]{:S(2)}, u32[]{:S(2)}) collective-permute-start(f32[3,64,256]{2,1,0:T(8,128)S(1)} %dynamic-slice_bitcast_fusion.7), channel_id=1, source_target_pairs={{0,1},{1,0},{2,3},{3,2},{4,5},{5,4},{6,7},{7,6},{8,9},{9,8},{10,11... | collective-permute-start | bytes 589832 | tf_op jit(solution)/shard_map/ppermute | solution.py:101
  298.2 1.8 copy-start.19
  298.3 14.7 %collective-permute-start.22 = (f32[1,64,2048]{2,1,0:T(8,128)S(1)}, f32[1,64,2048]{2,1,0:T(8,128)S(1)}, u32[]{:S(2)}, u32[]{:S(2)}) collective-permute-start(f32[1,64,2048]{2,1,0:T(8,128)S(1)} %dynamic-slice_bitcast_fusion.3), channel_id=1, source_target_pairs={{0,1},{1,0},{2,3},{3,2},{4,5},{5,4},{6,7},{7,6},{8,9},{9,8},{10,11... | collective-permute-start | bytes 1572872 | tf_op jit(solution)/shard_map/ppermute | solution.py:101
  301.2 21.8 %collective-permute-start.28 = (f32[128,128]{1,0:T(8,128)S(1)}, f32[128,128]{1,0:T(8,128)S(1)}, u32[]{:S(2)}, u32[]{:S(2)}) collective-permute-start(f32[128,128]{1,0:T(8,128)S(1)} %fusion.2), channel_id=1, source_target_pairs={{1,0},{3,2},{5,4},{7,6},{9,16},{11,18},{13,20},{15,22},{17,9},{19,... | collective-permute-start | bytes 196616 | tf_op jit(solution)/shard_map/ppermute | solution.py:146
  302.5 21.9 %collective-permute-start.26 = (f32[128,128]{1,0:T(8,128)S(1)}, f32[128,128]{1,0:T(8,128)S(1)}, u32[]{:S(2)}, u32[]{:S(2)}) collective-permute-start(f32[128,128]{1,0:T(8,128)S(1)} %fusion.2), channel_id=1, source_target_pairs={{0,0},{2,2},{4,4},{6,6},{8,16},{10,18},{12,20},{14,22},{16,9},{18,... | collective-permute-start | bytes 196616 | tf_op jit(solution)/shard_map/ppermute | solution.py:146
  314.7 29.1 %copy-start.25 = (f32[256,128]{1,0:T(8,128)S(1)}, f32[256,128]{1,0:T(8,128)}, u32[]{:S(2)}) copy-start(f32[256,128]{1,0:T(8,128)} %add.185) | copy-start | bytes 393220
  314.7 9.7 %collective-permute-start.29 = (f32[128,128]{1,0:T(8,128)S(1)}, f32[128,128]{1,0:T(8,128)S(1)}, u32[]{:S(2)}, u32[]{:S(2)}) collective-permute-start(f32[128,128]{1,0:T(8,128)S(1)} %fusion), channel_id=1, source_target_pairs={{1,8},{3,10},{5,12},{7,14},{9,24},{11,26},{13,28},{15,30},{17,1},{... | collective-permute-start | bytes 196616 | tf_op jit(solution)/shard_map/ppermute | solution.py:146
  315.7 8.7 %collective-permute-start.27 = (f32[128,128]{1,0:T(8,128)S(1)}, f32[128,128]{1,0:T(8,128)S(1)}, u32[]{:S(2)}, u32[]{:S(2)}) collective-permute-start(f32[128,128]{1,0:T(8,128)S(1)} %fusion), channel_id=1, source_target_pairs={{0,8},{2,10},{4,12},{6,14},{8,24},{10,26},{12,28},{14,30},{16,1},{... | collective-permute-start | bytes 196616 | tf_op jit(solution)/shard_map/ppermute | solution.py:146
  322.4 22.1 %collective-permute-start.25 = (bf16[128,2048]{1,0:T(8,128)(2,1)S(1)}, bf16[128,2048]{1,0:T(8,128)(2,1)S(1)}, u32[]{:S(2)}, u32[]{:S(2)}) collective-permute-start(bf16[128,2048]{1,0:T(8,128)(2,1)S(1)} %get-tuple-element.90), channel_id=1, source_target_pairs={{1,8},{3,10},{5,12},{7,14},{9,24},{11,26},{13,28},{15,30},{17,1},{... | collective-permute-start | bytes 1572872 | tf_op jit(solution)/shard_map/ppermute | solution.py:146
  323.1 25.9 %collective-permute-start.24 = (bf16[128,2048]{1,0:T(8,128)(2,1)S(1)}, bf16[128,2048]{1,0:T(8,128)(2,1)S(1)}, u32[]{:S(2)}, u32[]{:S(2)}) collective-permute-start(bf16[128,2048]{1,0:T(8,128)(2,1)S(1)} %get-tuple-element.91), channel_id=1, source_target_pairs={{1,0},{3,2},{5,4},{7,6},{9,16},{11,18},{13,20},{15,22},{17,9},{19,... | collective-permute-start | bytes 1572872 | tf_op jit(solution)/shard_map/ppermute | solution.py:146
  324.5 19.2 %collective-permute-start.30 = (f32[256,128]{1,0:T(8,128)S(1)}, f32[256,128]{1,0:T(8,128)S(1)}, u32[]{:S(2)}, u32[]{:S(2)}) collective-permute-start(f32[256,128]{1,0:T(8,128)S(1)} %pad_maximum_fusion.19), channel_id=1, source_target_pairs={{0,1},{1,0},{2,3},{3,2},{4,5},{5,4},{6,7},{7,6},{8,9},{9,8},{10,11... | collective-permute-start | bytes 393224 | tf_op jit(solution)/shard_map/ppermute | solution.py:167
  330.9 18.3 %collective-permute-start.23 = (bf16[128,2048]{1,0:T(8,128)(2,1)S(1)}, bf16[128,2048]{1,0:T(8,128)(2,1)S(1)}, u32[]{:S(2)}, u32[]{:S(2)}) collective-permute-start(bf16[128,2048]{1,0:T(8,128)(2,1)S(1)} %get-tuple-element.90), channel_id=1, source_target_pairs={{0,8},{2,10},{4,12},{6,14},{8,24},{10,26},{12,28},{14,30},{16,1},{... | collective-permute-start | bytes 1572872 | tf_op jit(solution)/shard_map/ppermute | solution.py:146
  332.2 21.2 %collective-permute-start.20 = (bf16[128,2048]{1,0:T(8,128)(2,1)S(1)}, bf16[128,2048]{1,0:T(8,128)(2,1)S(1)}, u32[]{:S(2)}, u32[]{:S(2)}) collective-permute-start(bf16[128,2048]{1,0:T(8,128)(2,1)S(1)} %get-tuple-element.91), channel_id=1, source_target_pairs={{0,0},{2,2},{4,4},{6,6},{8,16},{10,18},{12,20},{14,22},{16,9},{18,... | collective-permute-start | bytes 1572872 | tf_op jit(solution)/shard_map/ppermute | solution.py:146
  349.1 5.4 %copy-start.1 = (bf16[8192,128]{1,0:T(8,128)(2,1)S(1)}, bf16[8192,128]{1,0:T(8,128)(2,1)}, u32[]{:S(2)}) copy-start(bf16[8192,128]{1,0:T(8,128)(2,1)} %param.4) | copy-start | bytes 6291460
  (1 other events, 1.0 us)
Sparse Core Ops, SparseCore 0:
  162.1 20.1 all-gather.1

commit v4 on v2

--- a/solution.py
+++ b/solution.py
@@ -84,59 +84,72 @@
         axis_index_groups=[list(range(half)), list(range(half, 2 * half))],
     )
 
-    def summed(tile):
+    def shared(tile, index, name, swap):
         rows = tile.shape[0] // 2
-        keep = lax.dynamic_slice_in_dim(tile, core * rows, rows, 0)
-        send = lax.dynamic_slice_in_dim(tile, (1 - core) * rows, rows, 0)
-        tile = keep + lax.ppermute(send, "dp", core_swap)
-        rows = rows // 2
-        keep = lax.dynamic_slice_in_dim(tile, feat_index * rows, rows, 0)
-        send = lax.dynamic_slice_in_dim(tile, (1 - feat_index) * rows, rows, 0)
-        return keep + lax.ppermute(send, "feat", feat_swap)
+        keep = lax.dynamic_slice_in_dim(tile, index * rows, rows, 0)
+        send = lax.dynamic_slice_in_dim(tile, (1 - index) * rows, rows, 0)
+        return keep + lax.ppermute(send, name, swap)
+
+    def core_sum(tile):
+        return shared(tile, core, "dp", core_swap)
+
+    def feat_sum(tile):
+        return shared(tile, feat_index, "feat", feat_swap)
+
+    def products(rows, chips):
+        return jnp.concatenate([pair_tile(rows, cols) for cols in chips], 1)
 
     rows_a = jnp.where(is_inner, near, own)
-    early = summed(
-        jnp.concatenate([pair_tile(rows_a, cols) for cols in (own, by_side, by_part)], 1)
-    )
+    early = feat_sum(core_sum(products(rows_a, (own, by_side, by_part))))
     far, by_both, early, first_half = lax.optimization_barrier((far, by_both, early, first_half))
     rows_b = jnp.where(is_inner, far, by_part)
-    late_b = summed(
-        jnp.concatenate([pair_tile(rows_b, cols) for cols in (own, by_side, by_part, by_both)], 1)
-    )
-    late_a = summed(pair_tile(rows_a, by_both))
-    gram = jnp.concatenate([jnp.concatenate([early, late_a], 1), late_b], 0)
+    b_low = core_sum(products(rows_b, (own, by_side)))
+    late_a = feat_sum(core_sum(pair_tile(rows_a, by_both)))
+    b_low, by_part_late, by_both_late = lax.optimization_barrier((b_low, by_part, by_both))
+    b_high = core_sum(products(rows_b, (by_part_late, by_both_late)))
+    late_b = [feat_sum(b_low), feat_sum(b_high)]
 
-    chip_cols = own.shape[0]
-    own_x, side_x, part_x, both_x = (
-        gram[:, i * chip_cols:(i + 1) * chip_cols] for i in range(4)
-    )
-    gram_cols = ordered(
-        part % 2,
-        ordered(side, own_x, side_x, 1),
-        ordered(side, part_x, both_x, 1),
-        1,
-    )
     rows_of = jnp.asarray(ROWS_OF, jnp.int32)[part]
     piece = row_count // 2
-    row_base = ((rows_of * 2 + side) * 2 + core) * row_count + feat_index * piece
-    row_ids = (row_base[:, None] + jnp.arange(piece, dtype=jnp.int32)[None, :]).reshape(-1)
-    col_count = gram_cols.shape[1]
-    col_ids = (part // 2) * col_count + jnp.arange(col_count, dtype=jnp.int32)
-    pair_values = jnp.where(row_ids[:, None] == col_ids[None, :], 0.0, gram_cols)
-    partial_sum = jnp.dot(pair_values, first_half, precision=lax.Precision.HIGHEST)
 
-    def deliver(values):
-        out = []
-        for flip in (0, 1):
-            sent = jnp.where((feat_index ^ flip) == 0, values[:piece], values[piece:])
-            out.append(lax.ppermute(sent, both, [
-                (at(p, s, c) * 2 + f, at(ROWS_OF[p][f ^ flip], s, c) * 2 + p // 2)
-                for p in range(4) for s in (0, 1) for c in (0, 1) for f in (0, 1)
-            ]))
-        return ordered((part + feat_index) % 2, out[0], out[1], 0)
+    def finished(tile, which):
+        col_count = tile.shape[1]
+        chip_cols = own.shape[0]
+        own_x, side_x, part_x, both_x = (
+            tile[:, i * chip_cols:(i + 1) * chip_cols] for i in range(4)
+        )
+        tile = ordered(
+            part % 2, ordered(side, own_x, side_x, 1), ordered(side, part_x, both_x, 1), 1
+        )
+        row_base = ((rows_of[which] * 2 + side) * 2 + core) * row_count + feat_index * piece
+        row_ids = row_base + jnp.arange(piece, dtype=jnp.int32)
+        col_ids = (part // 2) * col_count + jnp.arange(col_count, dtype=jnp.int32)
+        return jnp.where(row_ids[:, None] == col_ids[None, :], 0.0, tile)
 
-    half_sum = deliver(partial_sum)
-    interactions = deliver(pair_values.astype(jnp.bfloat16))
+    def weighted(values):
+        return jnp.dot(values, first_half, precision=lax.Precision.HIGHEST)
+
+    def deliver(values, which):
+        return [
+            lax.ppermute(values, both, [
+                (at(p, s, c) * 2 + f, at(ROWS_OF[p][which], s, c) * 2 + p // 2)
+                for p in range(4) for s in (0, 1) for c in (0, 1)
+            ])
+            for f in (0, 1)
+        ]
+
+    takes_a = (part + feat_index) % 2 == 0
+
+    def placed(from_a, from_b):
+        return jnp.concatenate([jnp.where(takes_a, a, b) for a, b in zip(from_a, from_b)], 0)
+
+    values_a = finished(jnp.concatenate([early, late_a], 1), 0)
+    sent_a = deliver(values_a.astype(jnp.bfloat16), 0)
+    sent_sums_a = deliver(weighted(values_a), 0)
+    sent_a, sent_sums_a, late_b = lax.optimization_barrier((sent_a, sent_sums_a, late_b))
+    values_b = finished(jnp.concatenate(late_b, 1), 1)
+    half_sum = placed(sent_sums_a, deliver(weighted(values_b), 1))
+    interactions = placed(sent_a, deliver(values_b.astype(jnp.bfloat16), 1))
     pair_sum = half_sum + lax.ppermute(half_sum, "feat", feat_swap)
     return (interactions, first_local - pair_weight * pair_sum)
 

time: 331 us -> 337 us (1.018); the launches traced: 331 us -> 333 us
  waiting for transfers between devices: 206 us -> 197 us
  starting transfers between devices: 29.4 us -> 37.5 us
    ppermute x10 -> x16, waiting for transfers between devices: 58.1 us -> 49.2 us  [the longest x8 48 us: shared(): return keep + lax.ppermute(send, name, swap)]
    ppermute x10 -> x16, starting transfers between devices: 20.1 us -> 26 us  [the longest x8 19.6 us: deliver(): lax.ppermute(values, both, [(at(p, s, c) * 2 + f, at(ROWS_OF[p][which], s...]
    add x9 -> x10, other arithmetic: 8.82 us -> 7.09 us  [the longest x7 7.07 us: shared(): return keep + lax.ppermute(send, name, swap)]
    unnamed x31 -> x39, local copies, waits for them, and re-layouts: 7.8 us -> 7.36 us
  transfers between devices with their start and end apart: 19 -> 25, of which waited for: 10 -> 12; matrix products, arithmetic and copies ran while one was open for 11% -> 16% of each run, Pallas kernels for 0% -> 0%
where the time goes in v4:
time: 337 us; the launch traced here: 333 us
  waiting for transfers between devices  197 us (58%)
  matrix products  40 us (12%)
  starting transfers between devices  37.5 us (11%)
  other arithmetic  26.9 us (8%)
  between operations  16 us (5%)
  local copies, waits for them, and re-layouts  15.5 us (5%)
    ppermute x1, waiting for transfers between devices, split_body(): by_part = lax.ppermute(own, 'dp', part_swap)  81.9 us
    ppermute x8, waiting for transfers between devices, shared(): return keep + lax.ppermute(send, name, swap)  48 us
    ppermute x1, waiting for transfers between devices, split_body(): far = lax.ppermute(own_late, 'dp', far_move)  46.3 us
    dot_general x8, matrix products, pair_tile(): lax.dot_general(left_rows, right_rows, (((1,), (1,)), ((), ())), preferre...  34.5 us
    ppermute x8, starting transfers between devices, deliver(): lax.ppermute(values, both, [(at(p, s, c) * 2 + f, at(ROWS_OF[p][which], s...  19.6 us
    ppermute x1, waiting for transfers between devices, split_body(): pair_sum = half_sum + lax.ppermute(half_sum, 'feat', feat_swap)  10.1 us
    unnamed x39, local copies, waits for them, and re-layouts  7.36 us
    add x7, other arithmetic, shared(): return keep + lax.ppermute(send, name, swap)  7.07 us
  transfers between devices with their start and end apart: 25, of which 12 were waited for; matrix products, arithmetic and copies ran while one was open for 16% of the time, Pallas kernels for 0%

profile of v4, /device:TPU:18, one launch (start us, length us, event | category | flops | bytes accessed | tf_op | source)
XLA Modules:
  0.0 332.6 jit_solution(10039205130399664236)
XLA Ops:
  7.2 3.3 constant_dynamic-slice_fusion.6
  10.5 4.5 %collective-permute-done = bf16[256,4096]{1,0:T(8,128)(2,1)} collective-permute-done((bf16[256,4096]{1,0:T(8,128)(2,1)}, bf16[256,4096]{1,0:T(8,128)(2,1)}, u32[]{:S(2)}, u32[]{:S(2)}) %collective-permute-start) | collective-permute-done | bytes 2097184 | tf_op jit(solution)/shard_map/ppermute | solution.py:70
  15.0 3.4 %broadcast_select_fusion.3 = (bf16[256,4096]{1,0:T(8,128)(2,1)S(1)}, bf16[256,4096]{1,0:T(8,128)(2,1)S(1)}) fusion(bf16[256,4096]{1,0:T(8,128)(2,1)} %collective-permute-done, pred[]{:T(512)S(6)} %eq.65, bf16[256,8192]{1,0:T(8,128)(2,1)} %param.3, s32[]{:T(128)S(6)} %select_n.188), kind=kLoop, calls=%fused_computation.13 | loop fusion | flops 2097152 | bytes 8388613 | tf_op jit(solution)/shard_map/jit(_where)/select_n | solution.py:63
  18.4 2.5 pad_maximum_fusion
  21.5 1.1 copy-done.4
  22.5 1.6 collective-permute-start.1
  24.1 1.9 collective-permute-start.5
  26.6 1.2 fusion.27
  27.9 1.6 collective-permute-start.2
  29.5 3.5 %collective-permute-done.2 = f32[256,128]{1,0:T(8,128)S(1)} collective-permute-done((f32[256,128]{1,0:T(8,128)S(1)}, f32[256,128]{1,0:T(8,128)S(1)}, u32[]{:S(2)}, u32[]{:S(2)}) %collective-permute-start.2) | collective-permute-done | bytes 131104 | tf_op jit(solution)/shard_map/ppermute | solution.py:76
  32.9 0.7 add.148
  33.6 81.9 %collective-permute-done.1 = bf16[512,4096]{1,0:T(8,128)(2,1)} collective-permute-done((bf16[512,4096]{1,0:T(8,128)(2,1)}, bf16[512,4096]{1,0:T(8,128)(2,1)}, u32[]{:S(2)}, u32[]{:S(2)}) %collective-permute-start.1) | collective-permute-done | bytes 4194336 | tf_op jit(solution)/shard_map/ppermute | solution.py:72
  115.5 1.3 collective-permute-start.3
  117.4 1.3 collective-permute-done.5
  118.7 4.4 %broadcast_select_fusion.1 = bf16[512,4096]{1,0:T(8,128)(2,1)S(1)} fusion(bf16[512,4096]{1,0:T(8,128)(2,1)} %collective-permute-done.5, pred[]{:T(512)S(6)} %or.3, bf16[256,4096]{1,0:T(8,128)(2,1)} %copy-done.4, bf16[256,4096]{1,0:T(8,128)(2,1)} %copy-done.2), kind=kLoop, calls=%fused_computation.2 | loop fusion | flops 10485760 | bytes 12582913 | tf_op jit(solution)/shard_map/jit(_where)/select_n | solution.py:102
  123.1 2.5 fusion.25
  125.6 4.7 %fusion.29 = f32[512,512]{0,1:T(8,128)S(1)} fusion(bf16[512,4096]{1,0:T(8,128)(2,1)S(1)} %broadcast_select_fusion.1, bf16[512,4096]{1,0:T(8,128)(2,1)} %collective-permute-done.1), kind=kOutput, calls=%fused_computation.81 | convolution fusion | flops 2147483648 | bytes 9437184 | tf_op jit(solution)/shard_map/dot_general | solution.py:8
  130.4 4.7 %fusion.28 = f32[512,512]{0,1:T(8,128)S(1)} fusion(bf16[512,4096]{1,0:T(8,128)(2,1)S(1)} %broadcast_select_fusion.1, bf16[512,4096]{1,0:T(8,128)(2,1)} %collective-permute-done.6), kind=kOutput, calls=%fused_computation.80 | convolution fusion | flops 2147483648 | bytes 9437184 | tf_op jit(solution)/shard_map/dot_general | solution.py:8
  135.6 1.6 copy-done.8
  137.2 1.3 constant_dynamic-slice_fusion.5
  138.5 3.7 %collective-permute-done.7 = f32[256,1536]{0,1:T(8,128)} collective-permute-done((f32[256,1536]{0,1:T(8,128)}, f32[256,1536]{0,1:T(8,128)}, u32[]{:S(2)}, u32[]{:S(2)}) %collective-permute-start.7) | collective-permute-done | bytes 1572896 | tf_op jit(solution)/shard_map/ppermute | solution.py:91
  142.2 2.1 dynamic-slice_add_fusion
  144.3 1.1 copy-done.9
  145.5 0.9 constant_dynamic-slice_fusion.4
  146.4 1.5 collective-permute-start.8
  147.9 18.3 %collective-permute-done.8 = f32[128,1536]{0,1:T(8,128)S(1)} collective-permute-done((f32[128,1536]{0,1:T(8,128)}, f32[128,1536]{0,1:T(8,128)S(1)}, u32[]{:S(2)}, u32[]{:S(2)}) %collective-permute-start.8) | collective-permute-done | bytes 786464 | tf_op jit(solution)/shard_map/ppermute | solution.py:91
  166.2 2.1 dynamic-slice_add_fusion.1
  168.3 46.3 %collective-permute-done.3 = bf16[512,4096]{1,0:T(8,128)(2,1)} collective-permute-done((bf16[512,4096]{1,0:T(8,128)(2,1)}, bf16[512,4096]{1,0:T(8,128)(2,1)}, u32[]{:S(2)}, u32[]{:S(2)}) %collective-permute-start.3) | collective-permute-done | bytes 4194336 | tf_op jit(solution)/shard_map/ppermute | solution.py:79
  214.6 2.6 broadcast_select_fusion
  217.2 2.5 fusion.24
  219.8 4.7 %fusion.31 = f32[512,512]{0,1:T(8,128)S(1)} fusion(bf16[512,4096]{1,0:T(8,128)(2,1)S(1)} %broadcast_select_fusion, bf16[512,4096]{1,0:T(8,128)(2,1)} %collective-permute-done.6), kind=kOutput, calls=%fused_computation.83 | convolution fusion | flops 2147483648 | bytes 9437184 | tf_op jit(solution)/shard_map/dot_general | solution.py:8
  224.5 1.1 fusion.3
  225.6 0.7 constant_dynamic-slice_fusion.7
  227.6 6.1 %fusion.30 = f32[512,512]{0,1:T(8,128)S(1)} fusion(bf16[512,4096]{1,0:T(8,128)(2,1)} %copy-done.13, bf16[512,4096]{1,0:T(8,128)(2,1)} %collective-permute-done.4), kind=kOutput, calls=%fused_computation.82 | convolution fusion | flops 2147483648 | bytes 9437184 | tf_op jit(solution)/shard_map/dot_general | solution.py:8
  234.3 1.2 fusion.5
  235.5 0.8 copy-done.15
  236.3 4.6 %fusion.32 = f32[512,512]{0,1:T(8,128)S(1)} fusion(bf16[512,4096]{1,0:T(8,128)(2,1)S(1)} %copy-done.15, bf16[512,4096]{1,0:T(8,128)(2,1)} %collective-permute-done.1), kind=kOutput, calls=%fused_computation.84 | convolution fusion | flops 2147483648 | bytes 9437184 | tf_op jit(solution)/shard_map/dot_general | solution.py:8
  240.8 4.6 %fusion.33 = f32[512,512]{0,1:T(8,128)S(1)} fusion(bf16[512,4096]{1,0:T(8,128)(2,1)S(1)} %copy-done.15, bf16[512,4096]{1,0:T(8,128)(2,1)} %collective-permute-done.4), kind=kOutput, calls=%fused_computation.85 | convolution fusion | flops 2147483648 | bytes 9437184 | tf_op jit(solution)/shard_map/dot_general | solution.py:8
  245.4 1.1 fusion
  247.1 0.8 copy-done.17
  247.9 1.6 collective-permute-start.10
  250.2 6.0 %collective-permute-done.10 = f32[128,512]{0,1:T(8,128)S(1)} collective-permute-done((f32[128,512]{0,1:T(8,128)S(1)}, f32[128,512]{0,1:T(8,128)S(1)}, u32[]{:S(2)}, u32[]{:S(2)}) %collective-permute-start.10) | collective-permute-done | bytes 262176 | tf_op jit(solution)/shard_map/ppermute | solution.py:91
  256.2 1.0 slice_select_fusion.5
  257.4 1.2 constant_dynamic-slice_fusion.1
  258.5 1.6 collective-permute-start.16
  260.1 1.5 fusion.2
  262.3 0.7 fusion.9
  263.0 1.3 collective-permute-start.12
  264.3 5.4 %collective-permute-start.11 = (bf16[128,2048]{0,1:T(8,128)(2,1)S(1)}, bf16[128,2048]{0,1:T(8,128)(2,1)S(1)}, u32[]{:S(2)}, u32[]{:S(2)}) collective-permute-start(bf16[128,2048]{0,1:T(8,128)(2,1)S(1)} %fusion.9), channel_id=1, source_target_pairs={{0,0},{2,2},{4,4},{6,6},{8,16},{10,18},{12,20},{14,22},{16,9},{18,... | collective-permute-start | bytes 1572872 | tf_op jit(solution)/shard_map/ppermute | solution.py:134
  269.8 2.2 fusion.8
  271.9 1.3 collective-permute-start.14
  273.2 12.9 %collective-permute-done.16 = f32[128,1024]{0,1:T(8,128)S(1)} collective-permute-done((f32[128,1024]{0,1:T(8,128)S(1)}, f32[128,1024]{0,1:T(8,128)S(1)}, u32[]{:S(2)}, u32[]{:S(2)}) %collective-permute-start.16) | collective-permute-done | bytes 524320 | tf_op jit(solution)/shard_map/ppermute | solution.py:91
  286.1 2.2 collective-permute-start.13
  288.4 7.1 %collective-permute-done.18 = f32[128,1024]{0,1:T(8,128)S(1)} collective-permute-done((f32[128,1024]{0,1:T(8,128)S(1)}, f32[128,1024]{0,1:T(8,128)S(1)}, u32[]{:S(2)}, u32[]{:S(2)}) %collective-permute-start.18) | collective-permute-done | bytes 524320 | tf_op jit(solution)/shard_map/ppermute | solution.py:91
  295.8 2.2 fusion.6
  298.6 0.8 fusion.7
  299.4 5.8 %collective-permute-start.21 = (f32[128,128]{1,0:T(8,128)S(1)}, f32[128,128]{1,0:T(8,128)S(1)}, u32[]{:S(2)}, u32[]{:S(2)}) collective-permute-start(f32[128,128]{1,0:T(8,128)S(1)} %fusion.6), channel_id=1, source_target_pairs={{0,8},{2,10},{4,12},{6,14},{8,24},{10,26},{12,28},{14,30},{16,1},{... | collective-permute-start | bytes 196616 | tf_op jit(solution)/shard_map/ppermute | solution.py:134
  305.2 0.7 collective-permute-start.20
  305.9 1.1 collective-permute-done.21
  307.1 3.9 %collective-permute-start.23 = (f32[256,128]{1,0:T(8,128)S(1)}, f32[256,128]{1,0:T(8,128)S(1)}, u32[]{:S(2)}, u32[]{:S(2)}) collective-permute-start(f32[256,128]{1,0:T(8,128)S(1)} %pad_maximum_fusion.7), channel_id=1, source_target_pairs={{0,1},{1,0},{2,3},{3,2},{4,5},{5,4},{6,7},{7,6},{8,9},{9,8},{10,11... | collective-permute-start | bytes 393224 | tf_op jit(solution)/shard_map/ppermute | solution.py:153
  311.0 2.3 collective-permute-start.19
  313.3 10.1 %collective-permute-done.23 = f32[256,128]{1,0:T(8,128)S(1)} collective-permute-done((f32[256,128]{1,0:T(8,128)S(1)}, f32[256,128]{1,0:T(8,128)S(1)}, u32[]{:S(2)}, u32[]{:S(2)}) %collective-permute-start.23) | collective-permute-done | bytes 131104 | tf_op jit(solution)/shard_map/ppermute | solution.py:153
  323.4 0.7 multiply_subtract_fusion
  324.4 1.4 copy.5
  (77 shorter events, 6.1 us)
Async XLA Ops:
  7.2 19.5 %copy-start = (bf16[8192,128]{1,0:T(8,128)(2,1)S(1)}, bf16[8192,128]{1,0:T(8,128)(2,1)}, u32[]{:S(2)}) copy-start(bf16[8192,128]{1,0:T(8,128)(2,1)} %param.4) | copy-start | bytes 6291460
  7.2 161.1 %all-gather.2.cloned.1.call-start = ((), (), s32[]{:S(2)}) async-start(), calls=%async_computation | async-start | bytes 1179648 | tf_op jit(solution)/shard_map/all_gather | solution.py:82
  10.5 4.5 %collective-permute-start = (bf16[256,4096]{1,0:T(8,128)(2,1)}, bf16[256,4096]{1,0:T(8,128)(2,1)}, u32[]{:S(2)}, u32[]{:S(2)}) collective-permute-start(bf16[256,4096]{1,0:T(8,128)(2,1)} %constant_dynamic-slice_fusion.6), channel_id=1, source_target_pairs={{0,2},{2,0},{4,6},{6,4},{8,10},{10,8},{12,14},{14,12},{16,18},{18,... | collective-permute-start | bytes 6291464 | tf_op jit(solution)/shard_map/ppermute | solution.py:70
  18.4 3.1 copy-start.2
  18.4 4.1 %copy-start.4 = (bf16[256,4096]{1,0:T(8,128)(2,1)}, bf16[256,4096]{1,0:T(8,128)(2,1)S(1)}, u32[]{:S(2)}) copy-start(bf16[256,4096]{1,0:T(8,128)(2,1)S(1)} %get-tuple-element.37) | copy-start | bytes 6291460
  18.4 8.2 %copy-start.7 = (bf16[256,8192]{1,0:T(8,128)(2,1)S(1)}, bf16[256,8192]{1,0:T(8,128)(2,1)}, u32[]{:S(2)}) copy-start(bf16[256,8192]{1,0:T(8,128)(2,1)} %param.3) | copy-start | bytes 12582916
  22.5 92.9 %collective-permute-start.1 = (bf16[512,4096]{1,0:T(8,128)(2,1)}, bf16[512,4096]{1,0:T(8,128)(2,1)}, u32[]{:S(2)}, u32[]{:S(2)}) collective-permute-start(bf16[512,4096]{1,0:T(8,128)(2,1)} %pad_maximum_fusion), channel_id=1, source_target_pairs={{0,8},{2,10},{4,12},{6,14},{8,0},{10,2},{12,4},{14,6},{16,24},{18,... | collective-permute-start | bytes 12582920 | tf_op jit(solution)/shard_map/ppermute | solution.py:72
  24.1 94.5 %collective-permute-start.5 = (bf16[512,4096]{1,0:T(8,128)(2,1)}, bf16[512,4096]{1,0:T(8,128)(2,1)}, u32[]{:S(2)}, u32[]{:S(2)}) collective-permute-start(bf16[512,4096]{1,0:T(8,128)(2,1)} %pad_maximum_fusion), channel_id=1, source_target_pairs={{8,16},{10,18},{12,20},{14,22},{16,8},{18,10},{20,12},{22,14},{9,1... | collective-permute-start | bytes 12582920 | tf_op jit(solution)/shard_map/ppermute | solution.py:74
  26.0 104.3 %collective-permute-start.6 = (bf16[512,4096]{1,0:T(8,128)(2,1)}, bf16[512,4096]{1,0:T(8,128)(2,1)}, u32[]{:S(2)}, u32[]{:S(2)}) collective-permute-start(bf16[512,4096]{1,0:T(8,128)(2,1)} %pad_maximum_fusion), channel_id=1, source_target_pairs={{0,4},{2,6},{4,0},{6,2},{8,12},{10,14},{12,8},{14,10},{16,20},{18,... | collective-permute-start | bytes 12582920 | tf_op jit(solution)/shard_map/ppermute | solution.py:73
  27.9 5.0 %collective-permute-start.2 = (f32[256,128]{1,0:T(8,128)S(1)}, f32[256,128]{1,0:T(8,128)S(1)}, u32[]{:S(2)}, u32[]{:S(2)}) collective-permute-start(f32[256,128]{1,0:T(8,128)S(1)} %fusion.27), channel_id=1, source_target_pairs={{0,1},{1,0},{2,3},{3,2},{4,5},{5,4},{6,7},{7,6},{8,9},{9,8},{10,11... | collective-permute-start | bytes 393224 | tf_op jit(solution)/shard_map/ppermute | solution.py:76
  33.6 89.4 %copy-start.3 = (bf16[256,4096]{1,0:T(8,128)(2,1)S(1)}, bf16[256,4096]{1,0:T(8,128)(2,1)}, u32[]{:S(2)}) copy-start(bf16[256,4096]{1,0:T(8,128)(2,1)} %copy-done.2) | copy-start | bytes 6291460
  33.6 89.5 %copy-start.5 = (bf16[256,4096]{1,0:T(8,128)(2,1)S(1)}, bf16[256,4096]{1,0:T(8,128)(2,1)}, u32[]{:S(2)}) copy-start(bf16[256,4096]{1,0:T(8,128)(2,1)} %copy-done.4) | copy-start | bytes 6291460
  115.5 99.1 %collective-permute-start.3 = (bf16[512,4096]{1,0:T(8,128)(2,1)}, bf16[512,4096]{1,0:T(8,128)(2,1)}, u32[]{:S(2)}, u32[]{:S(2)}) collective-permute-start(bf16[512,4096]{1,0:T(8,128)(2,1)} %pad_maximum_fusion), channel_id=1, source_target_pairs={{0,16},{2,18},{4,20},{6,22},{24,8},{26,10},{28,12},{30,14},{1,17},... | collective-permute-start | bytes 12582920 | tf_op jit(solution)/shard_map/ppermute | solution.py:79
  116.8 97.8 %collective-permute-start.4 = (bf16[512,4096]{1,0:T(8,128)(2,1)}, bf16[512,4096]{1,0:T(8,128)(2,1)}, u32[]{:S(2)}, u32[]{:S(2)}) collective-permute-start(bf16[512,4096]{1,0:T(8,128)(2,1)} %collective-permute-done.1), channel_id=1, source_target_pairs={{0,4},{2,6},{4,0},{6,2},{8,12},{10,14},{12,8},{14,10},{16,20},{18,... | collective-permute-start | bytes 12582920 | tf_op jit(solution)/shard_map/ppermute | solution.py:80
  123.1 7.3 %copy-start.13 = (bf16[512,4096]{1,0:T(8,128)(2,1)}, bf16[512,4096]{1,0:T(8,128)(2,1)S(1)}, u32[]{:S(2)}) copy-start(bf16[512,4096]{1,0:T(8,128)(2,1)S(1)} %broadcast_select_fusion.1) | copy-start | bytes 12582916
  135.5 1.6 copy-start.8
  138.5 3.8 %collective-permute-start.7 = (f32[256,1536]{0,1:T(8,128)}, f32[256,1536]{0,1:T(8,128)}, u32[]{:S(2)}, u32[]{:S(2)}) collective-permute-start(f32[256,1536]{0,1:T(8,128)} %constant_dynamic-slice_fusion.5), channel_id=1, source_target_pairs={{0,2},{2,0},{4,6},{6,4},{8,10},{10,8},{12,14},{14,12},{16,18},{18,... | collective-permute-start | bytes 4718600 | tf_op jit(solution)/shard_map/ppermute | solution.py:91
  144.3 1.1 copy-start.9
  146.4 19.8 %collective-permute-start.8 = (f32[128,1536]{0,1:T(8,128)}, f32[128,1536]{0,1:T(8,128)S(1)}, u32[]{:S(2)}, u32[]{:S(2)}) collective-permute-start(f32[128,1536]{0,1:T(8,128)} %constant_dynamic-slice_fusion.4), channel_id=1, source_target_pairs={{0,1},{1,0},{2,3},{3,2},{4,5},{5,4},{6,7},{7,6},{8,9},{9,8},{10,11... | collective-permute-start | bytes 2359304 | tf_op jit(solution)/shard_map/ppermute | solution.py:91
  168.3 48.9 %copy-start.6 = (bf16[256,4096]{1,0:T(8,128)(2,1)S(1)}, bf16[256,4096]{1,0:T(8,128)(2,1)}, u32[]{:S(2)}) copy-start(bf16[256,4096]{1,0:T(8,128)(2,1)} %copy-done.4) | copy-start | bytes 6291460
  217.2 2.5 copy-start.14
  225.6 8.7 %collective-permute-start.15 = (f32[256,1024]{0,1:T(8,128)}, f32[256,1024]{0,1:T(8,128)S(1)}, u32[]{:S(2)}, u32[]{:S(2)}) collective-permute-start(f32[256,1024]{0,1:T(8,128)} %fusion.3), channel_id=1, source_target_pairs={{0,2},{2,0},{4,6},{6,4},{8,10},{10,8},{12,14},{14,12},{16,18},{18,... | collective-permute-start | bytes 3145736 | tf_op jit(solution)/shard_map/ppermute | solution.py:91
  233.7 2.6 copy-start.15
  233.7 13.3 %collective-permute-start.9 = (f32[256,512]{0,1:T(8,128)S(1)}, f32[256,512]{0,1:T(8,128)S(1)}, u32[]{:S(2)}, u32[]{:S(2)}) collective-permute-start(f32[256,512]{0,1:T(8,128)S(1)} %constant_dynamic-slice_fusion.3), channel_id=1, source_target_pairs={{0,2},{2,0},{4,6},{6,4},{8,10},{10,8},{12,14},{14,12},{16,18},{18,... | collective-permute-start | bytes 1572872 | tf_op jit(solution)/shard_map/ppermute | solution.py:91
  245.4 11.9 %copy-start.11 = (f32[512,512]{0,1:T(8,128)}, f32[512,512]{0,1:T(8,128)S(1)}, u32[]{:S(2)}) copy-start(f32[512,512]{0,1:T(8,128)S(1)} %fusion.33) | copy-start | bytes 3145732
  245.4 10.8 %copy-start.16 = (f32[128,1536]{0,1:T(8,128)S(1)}, f32[128,1536]{0,1:T(8,128)}, u32[]{:S(2)}) copy-start(f32[128,1536]{0,1:T(8,128)} %dynamic-slice_add_fusion.1) | copy-start | bytes 2359300
  246.5 13.6 %collective-permute-start.17 = (f32[256,1024]{0,1:T(8,128)}, f32[256,1024]{0,1:T(8,128)}, u32[]{:S(2)}, u32[]{:S(2)}) collective-permute-start(f32[256,1024]{0,1:T(8,128)} %fusion), channel_id=1, source_target_pairs={{0,2},{2,0},{4,6},{6,4},{8,10},{10,8},{12,14},{14,12},{16,18},{18,... | collective-permute-start | bytes 3145736 | tf_op jit(solution)/shard_map/ppermute | solution.py:91
  247.1 0.8 copy-start.17
  247.9 8.3 %collective-permute-start.10 = (f32[128,512]{0,1:T(8,128)S(1)}, f32[128,512]{0,1:T(8,128)S(1)}, u32[]{:S(2)}, u32[]{:S(2)}) collective-permute-start(f32[128,512]{0,1:T(8,128)S(1)} %constant_dynamic-slice_fusion.2), channel_id=1, source_target_pairs={{0,1},{1,0},{2,3},{3,2},{4,5},{5,4},{6,7},{7,6},{8,9},{9,8},{10,11... | collective-permute-start | bytes 786440 | tf_op jit(solution)/shard_map/ppermute | solution.py:91
  257.3 12.4 %copy-start.10 = (f32[2048,128]{1,0:T(8,128)S(1)}, f32[2048,128]{1,0:T(8,128)}, u32[]{:S(2)}) copy-start(f32[2048,128]{1,0:T(8,128)} %all-gather.2.cloned.1.call-done) | copy-start | bytes 3145732
  258.5 29.8 %copy-start.12 = (f32[256,1024]{0,1:T(8,128)S(1)}, f32[256,1024]{0,1:T(8,128)}, u32[]{:S(2)}) copy-start(f32[256,1024]{0,1:T(8,128)} %fusion.5) | copy-start | bytes 3145732
  258.5 27.6 %collective-permute-start.16 = (f32[128,1024]{0,1:T(8,128)S(1)}, f32[128,1024]{0,1:T(8,128)S(1)}, u32[]{:S(2)}, u32[]{:S(2)}) collective-permute-start(f32[128,1024]{0,1:T(8,128)S(1)} %constant_dynamic-slice_fusion.1), channel_id=1, source_target_pairs={{0,1},{1,0},{2,3},{3,2},{4,5},{5,4},{6,7},{7,6},{8,9},{9,8},{10,11... | collective-permute-start | bytes 1572872 | tf_op jit(solution)/shard_map/ppermute | solution.py:91
  261.7 33.8 %collective-permute-start.18 = (f32[128,1024]{0,1:T(8,128)S(1)}, f32[128,1024]{0,1:T(8,128)S(1)}, u32[]{:S(2)}, u32[]{:S(2)}) collective-permute-start(f32[128,1024]{0,1:T(8,128)S(1)} %constant_dynamic-slice_fusion), channel_id=1, source_target_pairs={{0,1},{1,0},{2,3},{3,2},{4,5},{5,4},{6,7},{7,6},{8,9},{9,8},{10,11... | collective-permute-start | bytes 1572872 | tf_op jit(solution)/shard_map/ppermute | solution.py:91
  263.0 32.6 %collective-permute-start.12 = (bf16[128,2048]{0,1:T(8,128)(2,1)S(1)}, bf16[128,2048]{0,1:T(8,128)(2,1)S(1)}, u32[]{:S(2)}, u32[]{:S(2)}) collective-permute-start(bf16[128,2048]{0,1:T(8,128)(2,1)S(1)} %fusion.9), channel_id=1, source_target_pairs={{1,0},{3,2},{5,4},{7,6},{9,16},{11,18},{13,20},{15,22},{17,9},{19,... | collective-permute-start | bytes 1572872 | tf_op jit(solution)/shard_map/ppermute | solution.py:134
  264.3 31.3 %collective-permute-start.11 = (bf16[128,2048]{0,1:T(8,128)(2,1)S(1)}, bf16[128,2048]{0,1:T(8,128)(2,1)S(1)}, u32[]{:S(2)}, u32[]{:S(2)}) collective-permute-start(bf16[128,2048]{0,1:T(8,128)(2,1)S(1)} %fusion.9), channel_id=1, source_target_pairs={{0,0},{2,2},{4,4},{6,6},{8,16},{10,18},{12,20},{14,22},{16,9},{18,... | collective-permute-start | bytes 1572872 | tf_op jit(solution)/shard_map/ppermute | solution.py:134
  271.9 23.6 %collective-permute-start.14 = (f32[128,128]{1,0:T(8,128)S(1)}, f32[128,128]{1,0:T(8,128)S(1)}, u32[]{:S(2)}, u32[]{:S(2)}) collective-permute-start(f32[128,128]{1,0:T(8,128)S(1)} %fusion.8), channel_id=1, source_target_pairs={{1,0},{3,2},{5,4},{7,6},{9,16},{11,18},{13,20},{15,22},{17,9},{19,... | collective-permute-start | bytes 196616 | tf_op jit(solution)/shard_map/ppermute | solution.py:134
  286.1 9.5 %collective-permute-start.13 = (f32[128,128]{1,0:T(8,128)S(1)}, f32[128,128]{1,0:T(8,128)S(1)}, u32[]{:S(2)}, u32[]{:S(2)}) collective-permute-start(f32[128,128]{1,0:T(8,128)S(1)} %fusion.8), channel_id=1, source_target_pairs={{0,0},{2,2},{4,4},{6,6},{8,16},{10,18},{12,20},{14,22},{16,9},{18,... | collective-permute-start | bytes 196616 | tf_op jit(solution)/shard_map/ppermute | solution.py:134
  295.6 27.8 %copy-start.18 = (f32[256,128]{1,0:T(8,128)S(1)}, f32[256,128]{1,0:T(8,128)}, u32[]{:S(2)}) copy-start(f32[256,128]{1,0:T(8,128)} %add.148) | copy-start | bytes 393220
  298.0 7.9 %collective-permute-start.22 = (f32[128,128]{1,0:T(8,128)S(1)}, f32[128,128]{1,0:T(8,128)S(1)}, u32[]{:S(2)}, u32[]{:S(2)}) collective-permute-start(f32[128,128]{1,0:T(8,128)S(1)} %fusion.6), channel_id=1, source_target_pairs={{1,8},{3,10},{5,12},{7,14},{9,24},{11,26},{13,28},{15,30},{17,1},{... | collective-permute-start | bytes 196616 | tf_op jit(solution)/shard_map/ppermute | solution.py:134
  299.4 7.7 %collective-permute-start.21 = (f32[128,128]{1,0:T(8,128)S(1)}, f32[128,128]{1,0:T(8,128)S(1)}, u32[]{:S(2)}, u32[]{:S(2)}) collective-permute-start(f32[128,128]{1,0:T(8,128)S(1)} %fusion.6), channel_id=1, source_target_pairs={{0,8},{2,10},{4,12},{6,14},{8,24},{10,26},{12,28},{14,30},{16,1},{... | collective-permute-start | bytes 196616 | tf_op jit(solution)/shard_map/ppermute | solution.py:134
  305.2 18.9 %collective-permute-start.20 = (bf16[128,2048]{0,1:T(8,128)(2,1)S(1)}, bf16[128,2048]{0,1:T(8,128)(2,1)S(1)}, u32[]{:S(2)}, u32[]{:S(2)}) collective-permute-start(bf16[128,2048]{0,1:T(8,128)(2,1)S(1)} %fusion.7), channel_id=1, source_target_pairs={{1,8},{3,10},{5,12},{7,14},{9,24},{11,26},{13,28},{15,30},{17,1},{... | collective-permute-start | bytes 1572872 | tf_op jit(solution)/shard_map/ppermute | solution.py:134
  305.9 19.9 %copy-start.1 = (bf16[8192,128]{1,0:T(8,128)(2,1)S(1)}, bf16[8192,128]{1,0:T(8,128)(2,1)}, u32[]{:S(2)}) copy-start(bf16[8192,128]{1,0:T(8,128)(2,1)} %param.4) | copy-start | bytes 6291460
  307.1 16.3 %collective-permute-start.23 = (f32[256,128]{1,0:T(8,128)S(1)}, f32[256,128]{1,0:T(8,128)S(1)}, u32[]{:S(2)}, u32[]{:S(2)}) collective-permute-start(f32[256,128]{1,0:T(8,128)S(1)} %pad_maximum_fusion.7), channel_id=1, source_target_pairs={{0,1},{1,0},{2,3},{3,2},{4,5},{5,4},{6,7},{7,6},{8,9},{9,8},{10,11... | collective-permute-start | bytes 393224 | tf_op jit(solution)/shard_map/ppermute | solution.py:153
  311.0 13.1 %collective-permute-start.19 = (bf16[128,2048]{0,1:T(8,128)(2,1)S(1)}, bf16[128,2048]{0,1:T(8,128)(2,1)S(1)}, u32[]{:S(2)}, u32[]{:S(2)}) collective-permute-start(bf16[128,2048]{0,1:T(8,128)(2,1)S(1)} %fusion.7), channel_id=1, source_target_pairs={{0,8},{2,10},{4,12},{6,14},{8,24},{10,26},{12,28},{14,30},{16,1},{... | collective-permute-start | bytes 1572872 | tf_op jit(solution)/shard_map/ppermute | solution.py:134
Sparse Core Ops, SparseCore 0:
  138.6 23.5 all-gather.1

commit v5 on v2

--- a/solution.py
+++ b/solution.py
@@ -26,6 +26,9 @@
     pair_values = jnp.where(row_ids[:, None] == col_ids[None, :], 0.0, gram_cols)
     first_all = lax.all_gather(first_local, "dp", axis=0, tiled=True)
     first_cols = lax.dynamic_slice_in_dim(first_all, feat_index * col_count, col_count, 0)
+    rounded, pair_values = lax.optimization_barrier(
+        (pair_values.astype(jnp.bfloat16), pair_values)
+    )
     partial_sum = jnp.dot(pair_values, first_cols, precision=lax.Precision.HIGHEST)
     pair_sum = lax.psum(partial_sum, "feat")
     data_scores = first_local - pair_weight * pair_sum
@@ -60,6 +63,9 @@
     feat_swap = [(0, 1), (1, 0)]
 
     def ordered(flag, mine, other, axis):
+        if axis == 0:
+            first = (jnp.arange(2, dtype=jnp.int32) == flag)[:, None, None]
+            return jnp.where(first, mine[None], other[None]).reshape(-1, mine.shape[1])
         low = jnp.where(flag == 0, mine, other)
         high = jnp.where(flag == 0, other, mine)
         return jnp.concatenate([low, high], axis)
@@ -123,6 +129,9 @@
     col_count = gram_cols.shape[1]
     col_ids = (part // 2) * col_count + jnp.arange(col_count, dtype=jnp.int32)
     pair_values = jnp.where(row_ids[:, None] == col_ids[None, :], 0.0, gram_cols)
+    rounded, pair_values = lax.optimization_barrier(
+        (pair_values.astype(jnp.bfloat16), pair_values)
+    )
     partial_sum = jnp.dot(pair_values, first_half, precision=lax.Precision.HIGHEST)
 
     def deliver(values):
@@ -135,8 +144,8 @@
             ]))
         return ordered((part + feat_index) % 2, out[0], out[1], 0)
 
+    interactions = deliver(rounded)
     half_sum = deliver(partial_sum)
-    interactions = deliver(pair_values.astype(jnp.bfloat16))
     pair_sum = half_sum + lax.ppermute(half_sum, "feat", feat_swap)
     return (interactions, first_local - pair_weight * pair_sum)
 

time: 331 us -> 334 us (level)
  matrix products: 40 us -> 45.7 us
    select_n x0 -> x3, other arithmetic: none -> 6.06 us  [ordered(): return jnp.where(first, mine[None], other[None]).reshape(-1, mine.shape[1])]
    dot_general x8, matrix products: 34.9 us -> 40.9 us  [pair_tile(): lax.dot_general(left_rows, right_rows, (((1,), (1,)), ((), ())), preferre...]
    unnamed x31 -> x18, local copies, waits for them, and re-layouts: 7.8 us -> 3.65 us
    select_n x5 -> x2, other arithmetic: 3.79 us -> 0.33 us  [ordered(): low = jnp.where(flag == 0, mine, other)]
where the time goes in v5:
time: 334 us; the launch traced here: 333 us
  waiting for transfers between devices  206 us (62%)
  matrix products  45.7 us (14%)
  starting transfers between devices  29.4 us (9%)
  other arithmetic  24.4 us (7%)
  between operations  14.5 us (4%)
  local copies, waits for them, and re-layouts  12.4 us (4%)
    ppermute x1, waiting for transfers between devices, split_body(): by_part = lax.ppermute(own, 'dp', part_swap)  81.8 us
    ppermute x1, waiting for transfers between devices, split_body(): far = lax.ppermute(own_late, 'dp', far_move)  48.6 us
    ppermute x3, waiting for transfers between devices, summed(): return keep + lax.ppermute(send, 'feat', feat_swap)  45.5 us
    dot_general x8, matrix products, pair_tile(): lax.dot_general(left_rows, right_rows, (((1,), (1,)), ((), ())), preferre...  40.9 us
    ppermute x4, starting transfers between devices, deliver(): lax.ppermute(sent, both, [(at(p, s, c) * 2 + f, at(ROWS_OF[p][f ^ flip],...  15.8 us
    ppermute x1, waiting for transfers between devices, split_body(): pair_sum = half_sum + lax.ppermute(half_sum, 'feat', feat_swap)  9.52 us
    ppermute x4, waiting for transfers between devices, deliver(): lax.ppermute(sent, both, [(at(p, s, c) * 2 + f, at(ROWS_OF[p][f ^ flip],...  8.52 us
  transfers between devices with their start and end apart: 19, of which 10 were waited for; matrix products, arithmetic and copies ran while one was open for 11% of the time, Pallas kernels for 0%

profile of v5, /device:TPU:18, one launch (start us, length us, event | category | flops | bytes accessed | tf_op | source)
XLA Modules:
  0.0 332.9 jit_solution(13009944116831373617)
XLA Ops:
  7.2 4.8 %constant_dynamic-slice_fusion.7 = (bf16[256,4096]{1,0:T(8,128)(2,1)}, bf16[256,4096]{1,0:T(8,128)(2,1)}) fusion(bf16[256,8192]{1,0:T(8,128)(2,1)} %param.3, s32[]{:T(128)S(6)} %select_n.162, s32[]{:T(128)S(6)} %select_n.163), kind=kLoop, calls=%fused_computation.36 | loop fusion | bytes 8388616 | tf_op jit(solution)/shard_map/dynamic_slice | solution.py:74
  12.2 4.4 %collective-permute-done = bf16[256,4096]{1,0:T(8,128)(2,1)} collective-permute-done((bf16[256,4096]{1,0:T(8,128)(2,1)}, bf16[256,4096]{1,0:T(8,128)(2,1)}, u32[]{:S(2)}, u32[]{:S(2)}) %collective-permute-start) | collective-permute-done | bytes 2097184 | tf_op jit(solution)/shard_map/ppermute | solution.py:76
  16.6 4.8 %bitcast_select_fusion = bf16[512,4096]{1,0:T(8,128)(2,1)} fusion(pred[512]{0:T(512)(128)(4,1)S(1)} %broadcast_in_dim.113, bf16[256,4096]{1,0:T(8,128)(2,1)} %collective-permute-done, bf16[256,4096]{1,0:T(8,128)(2,1)} %get-tuple-element.22), kind=kLoop, calls=%fused_computation.1 | loop fusion | flops 2097152 | bytes 8389120 | tf_op jit(solution)/shard_map/jit(_where)/select_n | solution.py:68
  21.4 1.6 collective-permute-start.1
  23.0 1.9 collective-permute-start.5
  24.9 0.6 collective-permute-start.6
  25.5 1.3 fusion.10
  26.9 1.6 collective-permute-start.2
  28.4 3.5 %collective-permute-done.2 = f32[256,128]{1,0:T(8,128)S(1)} collective-permute-done((f32[256,128]{1,0:T(8,128)S(1)}, f32[256,128]{1,0:T(8,128)S(1)}, u32[]{:S(2)}, u32[]{:S(2)}) %collective-permute-start.2) | collective-permute-done | bytes 131104 | tf_op jit(solution)/shard_map/ppermute | solution.py:82
  31.9 0.7 add.162
  32.6 81.8 %collective-permute-done.1 = bf16[512,4096]{1,0:T(8,128)(2,1)} collective-permute-done((bf16[512,4096]{1,0:T(8,128)(2,1)}, bf16[512,4096]{1,0:T(8,128)(2,1)}, u32[]{:S(2)}, u32[]{:S(2)}) %collective-permute-start.1) | collective-permute-done | bytes 4194336 | tf_op jit(solution)/shard_map/ppermute | solution.py:78
  114.3 1.5 collective-permute-start.3
  115.8 0.6 collective-permute-start.4
  116.4 1.1 collective-permute-done.5
  117.5 2.6 broadcast_select_fusion.1
  120.2 6.3 %fusion.11 = f32[512,512]{0,1:T(8,128)S(1)} fusion(bf16[512,4096]{1,0:T(8,128)(2,1)S(1)} %broadcast_select_fusion.1, bf16[512,4096]{1,0:T(8,128)(2,1)} %bitcast_select_fusion), kind=kOutput, calls=%fused_computation.51 | convolution fusion | flops 2147483648 | bytes 9437184 | tf_op jit(solution)/shard_map/dot_general | solution.py:8
  126.4 4.7 %fusion.13 = f32[512,512]{0,1:T(8,128)S(1)} fusion(bf16[512,4096]{1,0:T(8,128)(2,1)S(1)} %broadcast_select_fusion.1, bf16[512,4096]{1,0:T(8,128)(2,1)} %collective-permute-done.1), kind=kOutput, calls=%fused_computation.53 | convolution fusion | flops 2147483648 | bytes 9437184 | tf_op jit(solution)/shard_map/dot_general | solution.py:8
  131.2 4.7 %fusion.12 = f32[512,512]{0,1:T(8,128)S(1)} fusion(bf16[512,4096]{1,0:T(8,128)(2,1)S(1)} %broadcast_select_fusion.1, bf16[512,4096]{1,0:T(8,128)(2,1)} %collective-permute-done.6), kind=kOutput, calls=%fused_computation.52 | convolution fusion | flops 2147483648 | bytes 9437184 | tf_op jit(solution)/shard_map/dot_general | solution.py:8
  135.9 0.3 pad_maximum_fusion.1
  136.3 1.6 copy-done.5
  137.9 0.2 constant_dynamic-slice_fusion.5
  138.2 3.5 %collective-permute-done.7 = f32[256,1536]{0,1:T(8,128)} collective-permute-done((f32[256,1536]{0,1:T(8,128)S(1)}, f32[256,1536]{0,1:T(8,128)}, u32[]{:S(2)}, u32[]{:S(2)}) %collective-permute-start.7) | collective-permute-done | bytes 1572896 | tf_op jit(solution)/shard_map/ppermute | solution.py:97
  141.7 2.1 dynamic-slice_add_fusion.1
  143.8 1.6 collective-permute-start.8
  145.4 18.2 %collective-permute-done.8 = f32[128,1536]{0,1:T(8,128)} collective-permute-done((f32[128,1536]{0,1:T(8,128)S(1)}, f32[128,1536]{0,1:T(8,128)}, u32[]{:S(2)}, u32[]{:S(2)}) %collective-permute-start.8) | collective-permute-done | bytes 786464 | tf_op jit(solution)/shard_map/ppermute | solution.py:101
  163.6 1.2 dynamic-slice_add_fusion.3
  164.8 48.6 %collective-permute-done.3 = bf16[512,4096]{1,0:T(8,128)(2,1)} collective-permute-done((bf16[512,4096]{1,0:T(8,128)(2,1)}, bf16[512,4096]{1,0:T(8,128)(2,1)}, u32[]{:S(2)}, u32[]{:S(2)}) %collective-permute-start.3) | collective-permute-done | bytes 4194336 | tf_op jit(solution)/shard_map/ppermute | solution.py:85
  213.4 2.6 broadcast_select_fusion
  216.1 4.7 %fusion.15 = f32[512,512]{0,1:T(8,128)S(1)} fusion(bf16[512,4096]{1,0:T(8,128)(2,1)S(1)} %broadcast_select_fusion, bf16[512,4096]{1,0:T(8,128)(2,1)} %bitcast_select_fusion), kind=kOutput, calls=%fused_computation.55 | convolution fusion | flops 2147483648 | bytes 9437184 | tf_op jit(solution)/shard_map/dot_general | solution.py:8
  220.8 5.0 %fusion.18 = f32[512,512]{0,1:T(8,128)S(1)} fusion(bf16[512,4096]{1,0:T(8,128)(2,1)S(1)} %broadcast_select_fusion, bf16[512,4096]{1,0:T(8,128)(2,1)} %collective-permute-done.4), kind=kOutput, calls=%fused_computation.58 | convolution fusion | flops 2147483648 | bytes 9437184 | tf_op jit(solution)/shard_map/dot_general | solution.py:8
  225.8 4.7 %fusion.16 = f32[512,512]{0,1:T(8,128)S(1)} fusion(bf16[512,4096]{1,0:T(8,128)(2,1)S(1)} %broadcast_select_fusion, bf16[512,4096]{1,0:T(8,128)(2,1)} %collective-permute-done.6), kind=kOutput, calls=%fused_computation.56 | convolution fusion | flops 2147483648 | bytes 9437184 | tf_op jit(solution)/shard_map/dot_general | solution.py:8
  230.5 4.7 %fusion.17 = f32[512,512]{0,1:T(8,128)S(1)} fusion(bf16[512,4096]{1,0:T(8,128)(2,1)S(1)} %broadcast_select_fusion, bf16[512,4096]{1,0:T(8,128)(2,1)} %collective-permute-done.1), kind=kOutput, calls=%fused_computation.57 | convolution fusion | flops 2147483648 | bytes 9437184 | tf_op jit(solution)/shard_map/dot_general | solution.py:8
  235.3 0.4 pad_maximum_fusion
  235.8 2.0 copy-done.2
  237.7 0.2 constant_dynamic-slice_fusion.1
  238.1 6.0 %fusion.14 = f32[512,512]{0,1:T(8,128)S(1)} fusion(bf16[512,4096]{1,0:T(8,128)(2,1)} %copy-done.6, bf16[512,4096]{1,0:T(8,128)(2,1)} %collective-permute-done.4), kind=kOutput, calls=%fused_computation.54 | convolution fusion | flops 2147483648 | bytes 9437184 | tf_op jit(solution)/shard_map/dot_general | solution.py:8
  244.1 0.5 collective-permute-start.9
  244.6 2.1 dynamic-slice_add_fusion
  246.7 1.0 constant_dynamic-slice_fusion
  247.8 1.5 collective-permute-start.12
  249.4 0.7 constant_dynamic-slice_fusion.2
  250.1 0.5 collective-permute-start.10
  250.6 0.7 fusion.8
  251.4 27.3 %collective-permute-done.10 = f32[128,512]{0,1:T(8,128)} collective-permute-done((f32[128,512]{0,1:T(8,128)}, f32[128,512]{0,1:T(8,128)}, u32[]{:S(2)}, u32[]{:S(2)}) %collective-permute-start.10) | collective-permute-done | bytes 262176 | tf_op jit(solution)/shard_map/ppermute | solution.py:101
  278.8 1.0 dynamic-slice_add_fusion.5
  279.7 1.3 dynamic-slice_add_fusion.2
  281.1 0.1 pad_maximum_fusion.2
  281.2 0.2 slice_select_fusion.3
  281.4 0.1 fusion.1
  281.6 1.0 fusion.9
  282.7 3.5 %fusion.19 = f32[256,128]{1,0:T(8,128)S(1)} fusion(f32[256,2048]{0,1:T(8,128)S(1)} %get-tuple-element.18, f32[2048,128]{1,0:T(8,128)S(1)} %copy-done.8), kind=kOutput, calls=%fused_computation.59 | convolution fusion | flops 805306368 | bytes 3276800 | tf_op jit(solution)/shard_map/dot_general | solution.py:135
  286.2 3.4 %collective-permute-start.15 = (f32[128,128]{1,0:T(8,128)S(1)}, f32[128,128]{1,0:T(8,128)S(1)}, u32[]{:S(2)}, u32[]{:S(2)}) collective-permute-start(f32[128,128]{1,0:T(8,128)S(1)} %get-tuple-element.32), channel_id=1, source_target_pairs={{0,0},{1,8},{2,2},{3,10},{4,4},{5,12},{6,6},{7,14},{8,16},{9,24},{... | collective-permute-start | bytes 196616 | tf_op jit(solution)/shard_map/ppermute | solution.py:141
  289.6 5.2 %collective-permute-start.16 = (f32[128,128]{1,0:T(8,128)S(1)}, f32[128,128]{1,0:T(8,128)S(1)}, u32[]{:S(2)}, u32[]{:S(2)}) collective-permute-start(f32[128,128]{1,0:T(8,128)S(1)} %get-tuple-element.33), channel_id=1, source_target_pairs={{0,8},{1,0},{2,10},{3,2},{4,12},{5,4},{6,14},{7,6},{8,24},{9,16},{... | collective-permute-start | bytes 196616 | tf_op jit(solution)/shard_map/ppermute | solution.py:141
  294.8 0.9 broadcast_select_fusion.3
  295.7 2.2 collective-permute-start.13
  297.9 4.9 %collective-permute-start.14 = (bf16[128,2048]{0,1:T(8,128)(2,1)}, bf16[128,2048]{0,1:T(8,128)(2,1)}, u32[]{:S(2)}, u32[]{:S(2)}) collective-permute-start(bf16[128,2048]{0,1:T(8,128)(2,1)} %get-tuple-element.31), channel_id=1, source_target_pairs={{0,8},{1,0},{2,10},{3,2},{4,12},{5,4},{6,14},{7,6},{8,24},{9,16},{... | collective-permute-start | bytes 1572872 | tf_op jit(solution)/shard_map/ppermute | solution.py:141
  303.0 0.1 bitcast_select_fusion.2
  303.1 1.6 collective-permute-start.17
  304.7 9.5 %collective-permute-done.17 = f32[256,128]{1,0:T(8,128)S(1)} collective-permute-done((f32[256,128]{1,0:T(8,128)S(1)}, f32[256,128]{1,0:T(8,128)S(1)}, u32[]{:S(2)}, u32[]{:S(2)}) %collective-permute-start.17) | collective-permute-done | bytes 131104 | tf_op jit(solution)/shard_map/ppermute | solution.py:149
  314.2 0.7 multiply_subtract_fusion
  314.9 0.2 copy.5
  315.1 8.5 %collective-permute-done.14 = bf16[128,2048]{0,1:T(8,128)(2,1)} collective-permute-done((bf16[128,2048]{0,1:T(8,128)(2,1)}, bf16[128,2048]{0,1:T(8,128)(2,1)}, u32[]{:S(2)}, u32[]{:S(2)}) %collective-permute-start.14) | collective-permute-done | bytes 524320 | tf_op jit(solution)/shard_map/ppermute | solution.py:141
  323.6 1.2 copy.6
  324.9 1.1 bitcast_select_fusion.1
  (41 shorter events, 0.8 us)
Async XLA Ops:
  7.2 18.3 %copy-start = (bf16[8192,128]{1,0:T(8,128)(2,1)S(1)}, bf16[8192,128]{1,0:T(8,128)(2,1)}, u32[]{:S(2)}) copy-start(bf16[8192,128]{1,0:T(8,128)(2,1)} %param.4) | copy-start | bytes 6291460
  7.2 157.6 %all-gather.2.cloned.1.call-start = ((), (), s32[]{:S(2)}) async-start(), calls=%async_computation | async-start | bytes 1179648 | tf_op jit(solution)/shard_map/all_gather | solution.py:88
  12.1 4.5 %collective-permute-start = (bf16[256,4096]{1,0:T(8,128)(2,1)}, bf16[256,4096]{1,0:T(8,128)(2,1)}, u32[]{:S(2)}, u32[]{:S(2)}) collective-permute-start(bf16[256,4096]{1,0:T(8,128)(2,1)} %get-tuple-element.23), channel_id=1, source_target_pairs={{0,2},{2,0},{4,6},{6,4},{8,10},{10,8},{12,14},{14,12},{16,18},{18,... | collective-permute-start | bytes 6291464 | tf_op jit(solution)/shard_map/ppermute | solution.py:76
  16.6 8.9 %copy-start.4 = (bf16[256,8192]{1,0:T(8,128)(2,1)S(1)}, bf16[256,8192]{1,0:T(8,128)(2,1)}, u32[]{:S(2)}) copy-start(bf16[256,8192]{1,0:T(8,128)(2,1)} %param.3) | copy-start | bytes 12582916
  21.4 92.9 %collective-permute-start.1 = (bf16[512,4096]{1,0:T(8,128)(2,1)}, bf16[512,4096]{1,0:T(8,128)(2,1)}, u32[]{:S(2)}, u32[]{:S(2)}) collective-permute-start(bf16[512,4096]{1,0:T(8,128)(2,1)} %bitcast_select_fusion), channel_id=1, source_target_pairs={{0,8},{2,10},{4,12},{6,14},{8,0},{10,2},{12,4},{14,6},{16,24},{18,... | collective-permute-start | bytes 12582920 | tf_op jit(solution)/shard_map/ppermute | solution.py:78
  23.0 94.5 %collective-permute-start.5 = (bf16[512,4096]{1,0:T(8,128)(2,1)}, bf16[512,4096]{1,0:T(8,128)(2,1)}, u32[]{:S(2)}, u32[]{:S(2)}) collective-permute-start(bf16[512,4096]{1,0:T(8,128)(2,1)} %bitcast_select_fusion), channel_id=1, source_target_pairs={{8,16},{10,18},{12,20},{14,22},{16,8},{18,10},{20,12},{22,14},{9,1... | collective-permute-start | bytes 12582920 | tf_op jit(solution)/shard_map/ppermute | solution.py:80
  24.9 106.3 %collective-permute-start.6 = (bf16[512,4096]{1,0:T(8,128)(2,1)}, bf16[512,4096]{1,0:T(8,128)(2,1)}, u32[]{:S(2)}, u32[]{:S(2)}) collective-permute-start(bf16[512,4096]{1,0:T(8,128)(2,1)} %bitcast_select_fusion), channel_id=1, source_target_pairs={{0,4},{2,6},{4,0},{6,2},{8,12},{10,14},{12,8},{14,10},{16,20},{18,... | collective-permute-start | bytes 12582920 | tf_op jit(solution)/shard_map/ppermute | solution.py:79
  26.9 5.0 %collective-permute-start.2 = (f32[256,128]{1,0:T(8,128)S(1)}, f32[256,128]{1,0:T(8,128)S(1)}, u32[]{:S(2)}, u32[]{:S(2)}) collective-permute-start(f32[256,128]{1,0:T(8,128)S(1)} %fusion.10), channel_id=1, source_target_pairs={{0,1},{1,0},{2,3},{3,2},{4,5},{5,4},{6,7},{7,6},{8,9},{9,8},{10,11... | collective-permute-start | bytes 393224 | tf_op jit(solution)/shard_map/ppermute | solution.py:82
  114.3 99.1 %collective-permute-start.3 = (bf16[512,4096]{1,0:T(8,128)(2,1)}, bf16[512,4096]{1,0:T(8,128)(2,1)}, u32[]{:S(2)}, u32[]{:S(2)}) collective-permute-start(bf16[512,4096]{1,0:T(8,128)(2,1)} %bitcast_select_fusion), channel_id=1, source_target_pairs={{0,16},{2,18},{4,20},{6,22},{24,8},{26,10},{28,12},{30,14},{1,17},... | collective-permute-start | bytes 12582920 | tf_op jit(solution)/shard_map/ppermute | solution.py:85
  115.8 97.6 %collective-permute-start.4 = (bf16[512,4096]{1,0:T(8,128)(2,1)}, bf16[512,4096]{1,0:T(8,128)(2,1)}, u32[]{:S(2)}, u32[]{:S(2)}) collective-permute-start(bf16[512,4096]{1,0:T(8,128)(2,1)} %collective-permute-done.1), channel_id=1, source_target_pairs={{0,4},{2,6},{4,0},{6,2},{8,12},{10,14},{12,8},{14,10},{16,20},{18,... | collective-permute-start | bytes 12582920 | tf_op jit(solution)/shard_map/ppermute | solution.py:86
  120.1 11.0 %copy-start.6 = (bf16[512,4096]{1,0:T(8,128)(2,1)}, bf16[512,4096]{1,0:T(8,128)(2,1)S(1)}, u32[]{:S(2)}) copy-start(bf16[512,4096]{1,0:T(8,128)(2,1)S(1)} %broadcast_select_fusion.1) | copy-start | bytes 12582916
  136.3 1.6 copy-start.5
  138.1 3.6 %collective-permute-start.7 = (f32[256,1536]{0,1:T(8,128)S(1)}, f32[256,1536]{0,1:T(8,128)}, u32[]{:S(2)}, u32[]{:S(2)}) collective-permute-start(f32[256,1536]{0,1:T(8,128)S(1)} %constant_dynamic-slice_fusion.5), channel_id=1, source_target_pairs={{0,2},{2,0},{4,6},{6,4},{8,10},{10,8},{12,14},{14,12},{16,18},{18,... | collective-permute-start | bytes 4718600 | tf_op jit(solution)/shard_map/ppermute | solution.py:97
  143.8 19.8 %collective-permute-start.8 = (f32[128,1536]{0,1:T(8,128)S(1)}, f32[128,1536]{0,1:T(8,128)}, u32[]{:S(2)}, u32[]{:S(2)}) collective-permute-start(f32[128,1536]{0,1:T(8,128)S(1)} %constant_dynamic-slice_fusion.4), channel_id=1, source_target_pairs={{0,1},{1,0},{2,3},{3,2},{4,5},{5,4},{6,7},{7,6},{8,9},{9,8},{10,11... | collective-permute-start | bytes 2359304 | tf_op jit(solution)/shard_map/ppermute | solution.py:101
  235.7 2.0 copy-start.2
  237.9 6.7 %collective-permute-start.11 = (f32[256,2048]{0,1:T(8,128)S(1)}, f32[256,2048]{0,1:T(8,128)}, u32[]{:S(2)}, u32[]{:S(2)}) collective-permute-start(f32[256,2048]{0,1:T(8,128)S(1)} %constant_dynamic-slice_fusion.1), channel_id=1, source_target_pairs={{0,2},{2,0},{4,6},{6,4},{8,10},{10,8},{12,14},{14,12},{16,18},{18,... | collective-permute-start | bytes 6291464 | tf_op jit(solution)/shard_map/ppermute | solution.py:97
  238.1 6.5 %copy-start.3 = (f32[512,2048]{0,1:T(8,128)S(1)}, f32[512,2048]{0,1:T(8,128)}, u32[]{:S(2)}) copy-start(f32[512,2048]{0,1:T(8,128)} %copy-done.2) | copy-start | bytes 12582916
  244.1 5.2 %collective-permute-start.9 = (f32[256,512]{0,1:T(8,128)S(1)}, f32[256,512]{0,1:T(8,128)S(1)}, u32[]{:S(2)}, u32[]{:S(2)}) collective-permute-start(f32[256,512]{0,1:T(8,128)S(1)} %constant_dynamic-slice_fusion.3), channel_id=1, source_target_pairs={{0,2},{2,0},{4,6},{6,4},{8,10},{10,8},{12,14},{14,12},{16,18},{18,... | collective-permute-start | bytes 1572872 | tf_op jit(solution)/shard_map/ppermute | solution.py:97
  247.8 32.0 %collective-permute-start.12 = (f32[128,2048]{0,1:T(8,128)}, f32[128,2048]{0,1:T(8,128)}, u32[]{:S(2)}, u32[]{:S(2)}) collective-permute-start(f32[128,2048]{0,1:T(8,128)} %constant_dynamic-slice_fusion), channel_id=1, source_target_pairs={{0,1},{1,0},{2,3},{3,2},{4,5},{5,4},{6,7},{7,6},{8,9},{9,8},{10,11... | collective-permute-start | bytes 3145736 | tf_op jit(solution)/shard_map/ppermute | solution.py:101
  250.1 28.6 %collective-permute-start.10 = (f32[128,512]{0,1:T(8,128)}, f32[128,512]{0,1:T(8,128)}, u32[]{:S(2)}, u32[]{:S(2)}) collective-permute-start(f32[128,512]{0,1:T(8,128)} %constant_dynamic-slice_fusion.2), channel_id=1, source_target_pairs={{0,1},{1,0},{2,3},{3,2},{4,5},{5,4},{6,7},{7,6},{8,9},{9,8},{10,11... | collective-permute-start | bytes 786440 | tf_op jit(solution)/shard_map/ppermute | solution.py:101
  281.4 1.2 copy-start.8
  282.6 31.6 %copy-start.7 = (f32[256,128]{1,0:T(8,128)S(1)}, f32[256,128]{1,0:T(8,128)}, u32[]{:S(2)}) copy-start(f32[256,128]{1,0:T(8,128)} %add.162) | copy-start | bytes 393220
  282.7 43.4 %copy-start.1 = (bf16[8192,128]{1,0:T(8,128)(2,1)S(1)}, bf16[8192,128]{1,0:T(8,128)(2,1)}, u32[]{:S(2)}) copy-start(bf16[8192,128]{1,0:T(8,128)(2,1)} %param.4) | copy-start | bytes 6291460
  286.2 16.8 %collective-permute-start.15 = (f32[128,128]{1,0:T(8,128)S(1)}, f32[128,128]{1,0:T(8,128)S(1)}, u32[]{:S(2)}, u32[]{:S(2)}) collective-permute-start(f32[128,128]{1,0:T(8,128)S(1)} %get-tuple-element.32), channel_id=1, source_target_pairs={{0,0},{1,8},{2,2},{3,10},{4,4},{5,12},{6,6},{7,14},{8,16},{9,24},{... | collective-permute-start | bytes 196616 | tf_op jit(solution)/shard_map/ppermute | solution.py:141
  289.6 13.4 %collective-permute-start.16 = (f32[128,128]{1,0:T(8,128)S(1)}, f32[128,128]{1,0:T(8,128)S(1)}, u32[]{:S(2)}, u32[]{:S(2)}) collective-permute-start(f32[128,128]{1,0:T(8,128)S(1)} %get-tuple-element.33), channel_id=1, source_target_pairs={{0,8},{1,0},{2,10},{3,2},{4,12},{5,4},{6,14},{7,6},{8,24},{9,16},{... | collective-permute-start | bytes 196616 | tf_op jit(solution)/shard_map/ppermute | solution.py:141
  295.7 19.2 %collective-permute-start.13 = (bf16[128,2048]{0,1:T(8,128)(2,1)S(1)}, bf16[128,2048]{0,1:T(8,128)(2,1)S(1)}, u32[]{:S(2)}, u32[]{:S(2)}) collective-permute-start(bf16[128,2048]{0,1:T(8,128)(2,1)S(1)} %get-tuple-element.30), channel_id=1, source_target_pairs={{0,0},{1,8},{2,2},{3,10},{4,4},{5,12},{6,6},{7,14},{8,16},{9,24},{... | collective-permute-start | bytes 1572872 | tf_op jit(solution)/shard_map/ppermute | solution.py:141
  297.9 25.7 %collective-permute-start.14 = (bf16[128,2048]{0,1:T(8,128)(2,1)}, bf16[128,2048]{0,1:T(8,128)(2,1)}, u32[]{:S(2)}, u32[]{:S(2)}) collective-permute-start(bf16[128,2048]{0,1:T(8,128)(2,1)} %get-tuple-element.31), channel_id=1, source_target_pairs={{0,8},{1,0},{2,10},{3,2},{4,12},{5,4},{6,14},{7,6},{8,24},{9,16},{... | collective-permute-start | bytes 1572872 | tf_op jit(solution)/shard_map/ppermute | solution.py:141
  303.1 11.2 %collective-permute-start.17 = (f32[256,128]{1,0:T(8,128)S(1)}, f32[256,128]{1,0:T(8,128)S(1)}, u32[]{:S(2)}, u32[]{:S(2)}) collective-permute-start(f32[256,128]{1,0:T(8,128)S(1)} %bitcast_select_fusion.2), channel_id=1, source_target_pairs={{0,1},{1,0},{2,3},{3,2},{4,5},{5,4},{6,7},{7,6},{8,9},{9,8},{10,11... | collective-permute-start | bytes 393224 | tf_op jit(solution)/shard_map/ppermute | solution.py:149
Sparse Core Ops, SparseCore 0:
  138.3 24.6 all-gather.1
